TPU v7x, 32 devices: a whole 2x2x4 slice. The times are simulated.
32 devices in a mesh: dp: 8 (over z, y), tp: 4 (over x, core).
Axes of the slice: x: 2, y: 2, z: 4, core: 2. Of those that a mesh axis runs over, the one named last changes fastest.
Arguments:
- x_in: bfloat16 [1024, 8, 768], P('tp', 'dp'), may hold values from -6 to 6
- segments: int32 [1024, 8], P(None, 'dp'), may hold values from 0 to 4, as said below
- w_qkv: bfloat16 [2, 768, 2304], replicated, may hold values from -0.21875 to 0.21875
- w_out: bfloat16 [2, 768, 768], replicated, may hold values from -0.875 to 0.875
- mix_pre: float32 [2, 12, 12], replicated, may hold values from -1.75 to 1.75
- mix_post: float32 [2, 12, 12], replicated, may hold values from -1.75 to 1.75
- gain_attn: float32 [2, 768], replicated, may hold values from 0.5 to 1.5
- gain_ffn: float32 [2, 768], replicated, may hold values from 0.5 to 1.5
- w_in: bfloat16 [2, 768, 3072], P(None, None, 'tp'), may hold values from -0.21875 to 0.21875
- w_down: bfloat16 [2, 3072, 768], P(None, 'tp'), may hold values from -0.109375 to 0.109375
- cotangent: bfloat16 [1024, 8, 768], P('tp', 'dp'), may hold values from -6 to 6
Outputs:
- y_out: bfloat16 [1024, 8, 768], P('tp', 'dp')
- grad_x: float32 [1024, 8, 768], P('tp', 'dp')
- grad_qkv: float32 [2, 768, 2304], replicated
- grad_out: float32 [2, 768, 768], replicated
- grad_mix_pre: float32 [2, 12, 12], replicated
- grad_mix_post: float32 [2, 12, 12], replicated
- grad_gain_attn: float32 [2, 768], replicated
- grad_gain_ffn: float32 [2, 768], replicated
- grad_in: float32 [2, 768, 3072], P(None, 'dp', 'tp')
- grad_down: float32 [2, 3072, 768], P(None, 'tp', 'dp')
Inputs may be any that keep to these rules, and one draw needn't show every extreme that they name: `segments`: along each sequence the ids start at 0 and rise by one at the first position of each document; every sequence holds five documents.
All inputs are finite; a program needn't handle non-finite values.
Results may differ from a plain program's by a relative error of at most 0.035.
Values may be sent and summed in bfloat16 or wider, within the bound.
No kernel may reach another device: no remote copies, remote signals or barrier semaphores. Data moves between devices by JAX's collectives and lax.ppermute only.
A program may use at most 256 MiB of HBM per device.

v0:
```python
import functools

import jax
import jax.numpy as jnp
from jax import lax
from jax.experimental import pallas as pl
from jax.experimental.pallas import tpu as pltpu
from jax.sharding import PartitionSpec as P

LAYERS = 2
EPSILON = 1e-06
NEGATIVE = -1e30
LOG2E = 1.4426950408889634
GROUPS = 4
PIECES = 8
GP = 4
GB = 4
VMEM = 60 * 1024 * 1024
MIDDLE = 40 * 1024 * 1024
SMALL = 18 * 1024 * 1024
F32 = jnp.float32
BF16 = jnp.bfloat16


def dot_nn(a, b):
    return lax.dot_general(a, b, (((1,), (0,)), ((), ())), preferred_element_type=F32)


def dot_nt(a, b):
    return lax.dot_general(a, b, (((1,), (1,)), ((), ())), preferred_element_type=F32)


def dot_tn(a, b):
    return lax.dot_general(a, b, (((0,), (0,)), ((), ())), preferred_element_type=F32)


def rms(values, gain):
    return values * lax.rsqrt(jnp.mean(values * values, -1, keepdims=True) + EPSILON) * gain


def rms_back(grad, values, gain):
    inv = lax.rsqrt(jnp.mean(values * values, -1, keepdims=True) + EPSILON)
    unit = values * inv
    scaled = grad * gain
    grad_values = (scaled - unit * jnp.mean(scaled * unit, -1, keepdims=True)) * inv
    return grad_values, jnp.sum(grad * unit, axis=0)


def whole(shape):
    return pl.BlockSpec(shape, lambda *_: (0,) * len(shape))


def layer_of(array, layer):
    shape = array.shape[1:]
    return pl.BlockSpec((1,) + shape, lambda *_: (layer,) + (0,) * len(shape))


def attn_fwd_body(blocks, heads, layer, plain, *refs):
    n_refs = refs[:blocks]
    x_hbm, wqkv_hbm, wout_hbm, tab_ref, gain_ref, qinfo_ref, kinfo_ref, at_ref = refs[blocks : blocks + 8]
    p_ref, u_ref, q_ref, k_hbm, v_hbm, ot_ref, n1t_hbm, xm_ref, n2_ref = refs[blocks + 8 : blocks + 17]
    bias_ref, acc_ref, k_ref, v_ref, n1t_ref, x_ref, wqkv_ref, wout_ref, sems = refs[blocks + 17 :]
    step = pl.program_id(0)
    rows, width = x_ref.shape
    q_cols, k_cols, v_cols = [slice(i * width, (i + 1) * width) for i in range(3)]
    weights = [
        pltpu.make_async_copy(wqkv_hbm.at[layer, :, cols], wqkv_ref.at[i], sems.at[i])
        for i, cols in enumerate((k_cols, v_cols, q_cols))
    ]
    last_used = [
        pltpu.make_async_copy(wout_hbm.at[layer], wout_ref, sems.at[3]),
        pltpu.make_async_copy(x_hbm, x_ref, sems.at[4]),
    ]
    early = [
        pltpu.make_async_copy(k_ref, k_hbm, sems.at[5]),
        pltpu.make_async_copy(v_ref, v_hbm, sems.at[6]),
    ]
    turned = pltpu.make_async_copy(n1t_ref, n1t_hbm, sems.at[7])
    half = rows // 2
    at = at_ref[0]

    def place(r, second):
        block = chunk_of(at ^ r, second, blocks, plain)
        return pl.ds(pl.multiple_of(block * half, half), half)

    @pl.when(step == 0)
    def _():
        for copy in weights + last_used:
            copy.start()
        for i, ref in enumerate((k_ref, v_ref)):
            weights[i].wait()
            for r in range(blocks):
                value = dot_nn(n_refs[r][...], wqkv_ref[i]).astype(BF16)
                ref[place(r, 0), :] = value[:half]
                ref[place(r, 1), :] = value[half:]
            early[i].start()
        weights[2].wait()
        n_second = n_refs[blocks - 1 if plain else 0]
        q_ref[:half] = dot_nn(n_refs[0][:half], wqkv_ref[2]).astype(BF16)
        q_ref[half:] = dot_nn(n_second[half:], wqkv_ref[2]).astype(BF16)
        ok = (qinfo_ref[:, 1:2] == kinfo_ref[1:2, :]) & (kinfo_ref[0:1, :] <= qinfo_ref[:, 0:1])
        bias_ref[...] = jnp.where(ok, 0.0, NEGATIVE)
        acc_ref[...] = jnp.zeros_like(acc_ref)

    def work(second, keys):
        here = pl.ds(pl.multiple_of(second * half, half), half)
        q = q_ref[here, :].astype(F32)
        gs = [step * GP + u for u in range(GP)]
        qm = jnp.concatenate([(q * (tab_ref[0, pl.ds(g, 1), :] * LOG2E)).astype(BF16) for g in gs], 0)
        m = dot_nt(qm, k_ref[:keys, :])
        bias = bias_ref[here, :keys]
        ps = []
        for u in range(GP):
            mu = m[u * half : (u + 1) * half] + bias
            e = jnp.exp2(mu - jnp.max(mu, -1, keepdims=True))
            p = (e * (1.0 / jnp.sum(e, -1, keepdims=True))).astype(BF16)
            p_ref[u, here, :keys] = p
            ps.append(p)
        ctx = dot_nn(jnp.concatenate(ps, 0), v_ref[:keys, :])
        total = acc_ref[here, :]
        for u in range(GP):
            cu = ctx[u * half : (u + 1) * half]
            u_ref[u, here, :] = cu.astype(BF16)
            total = total + cu * tab_ref[0, pl.ds(heads + gs[u], 1), :]
        acc_ref[here, :] = total

    for pairs in range(1, blocks + 1):
        late = at == blocks - pairs

        @pl.when(late | (at == pairs - 1))
        def _(pairs=pairs, late=late):
            work(late.astype(jnp.int32), 2 * pairs * half)

    @pl.when(step == 0)
    def _():
        for r in range(blocks):
            for second in range(2):
                n1t_ref[:, place(r, second)] = n_refs[r][second * half : (second + 1) * half, :].T
        turned.start()

    @pl.when(step == pl.num_programs(0) - 1)
    def _():
        o = acc_ref[...].astype(BF16)
        ot_ref[...] = o.T
        for copy in last_used + early + [turned]:
            copy.wait()
        xm = x_ref[...] + dot_nn(o, wout_ref[...])
        xm_ref[...] = xm
        n2_ref[...] = rms(xm, gain_ref[pl.ds(layer, 1), :]).astype(BF16)


def chunk_of(device, second, devices, plain):
    if not second:
        return 2 * device
    return 2 * device + 1 if plain else 2 * (devices - 1 - device) + 1


def attn_fwd(layer, plain, n_blocks, x, w_qkv, w_out, tab, gain, where):
    rows, width = x.shape
    blocks = len(n_blocks)
    heads = tab.shape[1] // 2
    keys = rows * blocks
    args = (*n_blocks, x, w_qkv, w_out, tab, gain, *where)
    in_specs = [whole(a.shape) for a in args]
    in_specs[blocks : blocks + 3] = [pl.BlockSpec(memory_space=pl.ANY)] * 3
    in_specs[blocks + 3] = layer_of(tab, layer)
    in_specs[-1] = pl.BlockSpec(memory_space=pltpu.SMEM)
    out = [
        ((heads, rows, keys), BF16),
        ((heads, rows, width), BF16),
        ((rows, width), BF16),
        ((keys, width), BF16),
        ((keys, width), BF16),
        ((width, rows), BF16),
        ((width, keys), BF16),
        ((rows, width), F32),
        ((rows, width), BF16),
    ]
    out_specs = [whole(s) for s, _ in out]
    out_specs[0] = pl.BlockSpec((GP, rows, keys), lambda i: (i, 0, 0))
    out_specs[1] = pl.BlockSpec((GP, rows, width), lambda i: (i, 0, 0))
    for i in (3, 4, 6):
        out_specs[i] = pl.BlockSpec(memory_space=pltpu.HBM)
    return pl.pallas_call(
        functools.partial(attn_fwd_body, blocks, heads, layer, plain),
        grid=(heads // GP,),
        in_specs=in_specs,
        out_specs=out_specs,
        out_shape=[jax.ShapeDtypeStruct(s, d) for s, d in out],
        scratch_shapes=[
            pltpu.VMEM((rows, keys), F32),
            pltpu.VMEM((rows, width), F32),
            pltpu.VMEM((keys, width), BF16),
            pltpu.VMEM((keys, width), BF16),
            pltpu.VMEM((width, keys), BF16),
            pltpu.VMEM((rows, width), F32),
            pltpu.VMEM((3, width, width), BF16),
            pltpu.VMEM((width, width), BF16),
            pltpu.SemaphoreType.DMA((8,)),
        ],
        compiler_params=pltpu.CompilerParams(vmem_limit_bytes=MIDDLE),
        cost_estimate=pl.CostEstimate(
            flops=2 * rows * keys * width * heads * 2, bytes_accessed=20_000_000, transcendentals=rows * keys * heads
        ),
        name="attn_fwd",
    )(*args)


def attn_bwd_body(heads, blocks, layer, parts, *refs):
    (ga_ref, wout_ref, q_ref, k_ref, v_ref, p_ref, u_ref, tab_ref, tabt_ref, place_ref) = refs[:10]
    wqkv_hbm, n1t_hbm, ot_hbm = refs[10:13]
    gn1_refs = refs[13 : 13 + blocks]
    grad_refs = refs[13 + blocks : 13 + blocks + 2 * parts]
    zpre_ref, zpost_ref = refs[13 + blocks + 2 * parts : 15 + blocks + 2 * parts]
    go_ref, got_ref, qt_ref, gq_acc, gk_acc, gv_acc, wqkv_ref, n1t_ref, ot_ref, sems = refs[15 + blocks + 2 * parts :]
    step = pl.program_id(0)
    rows, width = q_ref.shape

    late = [
        pltpu.make_async_copy(wqkv_hbm.at[layer], wqkv_ref, sems.at[0]),
        pltpu.make_async_copy(n1t_hbm, n1t_ref, sems.at[1]),
        pltpu.make_async_copy(ot_hbm, ot_ref, sems.at[2]),
    ]

    @pl.when(step == 0)
    def _():
        for copy in late:
            copy.start()
        go = dot_nt(ga_ref[...], wout_ref[0]).astype(BF16).astype(F32)
        go_ref[...] = go
        got_ref[...] = go.T
        qt_ref[...] = q_ref[...].astype(F32).T
        gq_acc[...] = jnp.zeros_like(gq_acc)
        gk_acc[...] = jnp.zeros_like(gk_acc)
        gv_acc[...] = jnp.zeros_like(gv_acc)
        zpre_ref[...] = jnp.zeros_like(zpre_ref)
        zpost_ref[...] = jnp.zeros_like(zpost_ref)

    half = rows // 2
    at = place_ref[1 + parts]
    lane = lax.broadcasted_iota(jnp.int32, tabt_ref.shape[1:], 1)
    gs = [step * GB + u for u in range(GB)]
    cols = []
    for g in gs:
        pre_col = jnp.sum(jnp.where(lane == g, tabt_ref[0], 0.0), 1, keepdims=True)
        post_col = jnp.sum(jnp.where(lane == heads + g, tabt_ref[0], 0.0), 1, keepdims=True)
        cols.append((pre_col, post_col))

    def work(second, keys):
        here = pl.ds(pl.multiple_of(second * half, half), half)
        go = go_ref[here, :]
        q = q_ref[here, :].astype(F32)
        mixed = [go * tab_ref[0, pl.ds(heads + g, 1), :] for g in gs]
        gp = dot_nt(jnp.concatenate([x.astype(BF16) for x in mixed], 0), v_ref[:keys, :])
        gms, ps, zposts = [], [], []
        for u in range(GB):
            ctx = u_ref[u, here, :].astype(F32)
            zposts.append(jnp.sum(ctx * go, axis=0, keepdims=True))
            delta = jnp.sum(ctx * mixed[u], axis=1, keepdims=True)
            p = p_ref[u, here, :keys]
            gms.append((p.astype(F32) * (gp[u * half : (u + 1) * half] - delta)).astype(BF16))
            ps.append(p)
        gm = jnp.concatenate(gms, 0)
        t = dot_nn(gm, k_ref[:keys, :])
        total = gq_acc[here, :]
        zpres = []
        for u in range(GB):
            tu = t[u * half : (u + 1) * half]
            zpres.append(jnp.sum(tu * q, axis=0, keepdims=True))
            total = total + tu * tab_ref[0, pl.ds(gs[u], 1), :]
        gq_acc[here, :] = total
        qm = jnp.concatenate([(qt_ref[:, here] * pre).astype(BF16) for pre, _ in cols], 1)
        gk_acc[:, :keys] += dot_nn(qm, gm)
        gm2 = jnp.concatenate([(got_ref[:, here] * post).astype(BF16) for _, post in cols], 1)
        gv_acc[:, :keys] += dot_nn(gm2, jnp.concatenate(ps, 0))
        return zpres, zposts

    for pairs in range(1, blocks + 1):
        is_late = at == blocks - pairs

        @pl.when(is_late | (at == pairs - 1))
        def _(pairs=pairs, is_late=is_late):
            zpres, zposts = work(is_late.astype(jnp.int32), 2 * pairs * half)
            for u, g in enumerate(gs):
                zpre_ref[pl.ds(g, 1), :] += zpres[u]
                zpost_ref[pl.ds(g, 1), :] += zposts[u]

    @pl.when(step == pl.num_programs(0) - 1)
    def _():
        for copy in late:
            copy.wait()
        gq = gq_acc[...].astype(BF16)
        gkt = gk_acc[...].astype(BF16)
        gvt = gv_acc[...].astype(BF16)
        ga = ga_ref[...]
        for r in range(blocks):
            there = [pl.ds(pl.multiple_of(chunk_of(at ^ r, x, blocks, False) * half, half), half) for x in range(2)]
            gk = jnp.concatenate([gk_acc[:, x].T.astype(BF16) for x in there], 0)
            gv = jnp.concatenate([gv_acc[:, x].T.astype(BF16) for x in there], 0)
            gn1 = dot_nt(gk, wqkv_ref[:, width : 2 * width]) + dot_nt(gv, wqkv_ref[:, 2 * width :])
            if r == 0:
                gn1 = gn1 + dot_nt(gq, wqkv_ref[:, :width])
            gn1_refs[r][...] = gn1.astype(BF16)
        hand = width // 2
        per = hand // PIECES
        own = [pl.ds(pl.multiple_of(chunk_of(at, x, blocks, False) * half, half), half) for x in range(2)]
        for side in range(2):
            core = place_ref[0] if side == 0 else 1 - place_ref[0]
            mine = pl.ds(pl.multiple_of(core * hand, hand), hand)
            n1t = n1t_ref[mine, :]
            n1t_own = jnp.concatenate([n1t_ref[mine, x] for x in own], 1)
            grads = (
                lambda: dot_nn(n1t_own, gq),
                lambda: dot_nt(n1t, gkt),
                lambda: dot_nt(n1t, gvt),
                lambda: dot_nn(ot_ref[mine, :], ga),
            )
            for index, grad in enumerate(grads):
                part = index * parts // len(grads)
                column = (index - part * (len(grads) // parts)) * width
                value = grad().astype(BF16)
                for piece in range(PIECES):
                    there = pl.multiple_of((piece ^ place_ref[1 + part]) * per, per)
                    grad_refs[2 * part + side][pl.ds(there, per), column : column + width] = value[
                        piece * per : (piece + 1) * per
                    ]


def attn_bwd(layer, blocks, ga, w_out, q, k, v, p, u, tab, tabt, place, w_qkv, n1t, ot):
    rows, width = q.shape
    keys = k.shape[0]
    heads = p.shape[0]
    parts = place.shape[0] - 2
    args = (ga, w_out, q, k, v, p, u, tab, tabt, place, w_qkv, n1t, ot)
    in_specs = [whole(a.shape) for a in args]
    in_specs[1] = layer_of(w_out, layer)
    in_specs[5] = pl.BlockSpec((GB, rows, keys), lambda i: (i, 0, 0))
    in_specs[6] = pl.BlockSpec((GB, rows, width), lambda i: (i, 0, 0))
    in_specs[7] = layer_of(tab, layer)
    in_specs[8] = layer_of(tabt, layer)
    in_specs[9] = pl.BlockSpec(memory_space=pltpu.SMEM)
    in_specs[10:13] = [pl.BlockSpec(memory_space=pl.ANY)] * 3
    out = (
        [((rows, width), BF16)] * blocks
        + [((width // 2, 4 // parts * width), BF16)] * (2 * parts)
        + [((heads, width), F32)] * 2
    )
    res = pl.pallas_call(
        functools.partial(attn_bwd_body, heads, blocks, layer, parts),
        grid=(heads // GB,),
        in_specs=in_specs,
        out_specs=[whole(s) for s, _ in out],
        out_shape=[jax.ShapeDtypeStruct(s, d) for s, d in out],
        scratch_shapes=[
            pltpu.VMEM((rows, width), F32),
            pltpu.VMEM((width, rows), F32),
            pltpu.VMEM((width, rows), F32),
            pltpu.VMEM((rows, width), F32),
            pltpu.VMEM((width, keys), F32),
            pltpu.VMEM((width, keys), F32),
            pltpu.VMEM(w_qkv.shape[1:], BF16),
            pltpu.VMEM(n1t.shape, BF16),
            pltpu.VMEM(ot.shape, BF16),
            pltpu.SemaphoreType.DMA((3,)),
        ],
        compiler_params=pltpu.CompilerParams(vmem_limit_bytes=VMEM),
        cost_estimate=pl.CostEstimate(
            flops=2 * rows * keys * width * heads * 4 * 2, bytes_accessed=20_000_000, transcendentals=0
        ),
        name="attn_bwd",
    )(*args)
    return res[:blocks], res[blocks:-2], res[-2], res[-1]


def expand_body(parts, place_ref, *refs):
    qkv_ref, out_ref = refs[-2:]
    width3 = qkv_ref.shape[2]
    inner = PIECES // GROUPS
    per = qkv_ref.shape[1] // inner
    column = 0
    for part, ref in enumerate(refs[:parts]):
        end = column + ref.shape[1]
        cut = min(end, width3)
        for piece in range(inner):
            here = slice(piece * per, (piece + 1) * per)
            there = piece ^ lax.rem(place_ref[1 + part], inner)
            value = ref[pl.ds(pl.multiple_of(there * per, per), per), :].astype(F32)
            qkv_ref[0, here, column:cut] = value[:, : cut - column]
            if end > width3:
                out_ref[0, here, :] = value[:, cut - column :]
        column = end


def expand(layer, side, place, halves, before=()):
    half = halves[0].shape[0]
    width = sum(h.shape[1] for h in halves) // 4
    per = half // GROUPS
    in_specs = []
    for part, array in enumerate(halves):

        def piece(i, place, part=part):
            return i ^ (place[1 + part] // (PIECES // GROUPS)), 0

        in_specs.append(pl.BlockSpec((per, array.shape[1]), piece))
    first = 1 + len(halves)
    in_specs += [pl.BlockSpec(memory_space=pl.ANY)] * len(before)

    def there(i, place):
        return layer, (place[0] ^ side) * GROUPS + i, 0

    return pl.pallas_call(
        functools.partial(expand_body, len(halves)),
        grid_spec=pltpu.PrefetchScalarGridSpec(
            num_scalar_prefetch=1,
            grid=(GROUPS,),
            in_specs=in_specs,
            out_specs=[pl.BlockSpec((1, per, 3 * width), there), pl.BlockSpec((1, per, width), there)],
        ),
        out_shape=[
            jax.ShapeDtypeStruct((LAYERS, 2 * half, 3 * width), F32),
            jax.ShapeDtypeStruct((LAYERS, 2 * half, width), F32),
        ],
        input_output_aliases={first + i: i for i in range(len(before))},
        compiler_params=pltpu.CompilerParams(vmem_limit_bytes=SMALL),
        cost_estimate=pl.CostEstimate(flops=0, bytes_accessed=7_000_000, transcendentals=0),
        name="expand",
    )(place, *halves, *before)


def ffn_fwd_body(blocks, *refs):
    n_refs = refs[:blocks]
    win_ref, wdown_ref = refs[blocks : blocks + 2]
    out_refs = refs[blocks + 2 : 2 * blocks + 2]
    hid_ref, dgelu_ref = refs[2 * blocks + 2 :]
    rows = n_refs[0].shape[0]
    for r in range(blocks):
        here = pl.ds(r * rows, rows)
        pre = dot_nn(n_refs[r][...], win_ref[0])
        cdf = 0.5 + 0.5 * lax.erf(pre * (0.5**0.5))
        hid = (pre * cdf).astype(BF16)
        hid_ref[here, :] = hid
        density = jnp.exp2(pre * pre * (-0.5 * LOG2E)) * 0.3989422804014327
        dgelu_ref[here, :] = (cdf + pre * density).astype(BF16)
        out_refs[r][...] = dot_nn(hid, wdown_ref[0]).astype(BF16)


def ffn_fwd(layer, n_blocks, w_in, w_down):
    blocks = len(n_blocks)
    rows, width = n_blocks[0].shape
    hidden = w_in.shape[2]
    args = (*n_blocks, w_in, w_down)
    in_specs = [whole(a.shape) for a in args]
    in_specs[blocks] = layer_of(w_in, layer)
    in_specs[blocks + 1] = layer_of(w_down, layer)
    out = [((rows, width), BF16)] * blocks + [((rows * blocks, hidden), BF16)] * 2
    res = pl.pallas_call(
        functools.partial(ffn_fwd_body, blocks),
        grid=(1,),
        in_specs=in_specs,
        out_specs=[whole(s) for s, _ in out],
        out_shape=[jax.ShapeDtypeStruct(s, d) for s, d in out],
        compiler_params=pltpu.CompilerParams(vmem_limit_bytes=SMALL),
        cost_estimate=pl.CostEstimate(
            flops=4 * rows * blocks * width * hidden, bytes_accessed=6_000_000, transcendentals=rows * blocks * hidden
        ),
        name="ffn_fwd",
    )(*args)
    return res[:blocks], res[blocks], res[blocks + 1]


def ffn_bwd_body(blocks, *refs):
    g_refs = refs[:blocks]
    dgelu_ref, win_ref, wdown_ref = refs[blocks : blocks + 3]
    out_refs = refs[blocks + 3 : 2 * blocks + 3]
    gpre_ref = refs[2 * blocks + 3]
    rows = g_refs[0].shape[0]
    for r in range(blocks):
        here = pl.ds(r * rows, rows)
        gh = dot_nt(g_refs[r][...], wdown_ref[0])
        gpre = (gh * dgelu_ref[here, :].astype(F32)).astype(BF16)
        gpre_ref[here, :] = gpre
        out_refs[r][...] = dot_nt(gpre, win_ref[0]).astype(BF16)


def ffn_bwd(layer, g_blocks, dgelu, w_in, w_down):
    blocks = len(g_blocks)
    rows, width = g_blocks[0].shape
    hidden = w_in.shape[2]
    args = (*g_blocks, dgelu, w_in, w_down)
    in_specs = [whole(a.shape) for a in args]
    in_specs[blocks + 1] = layer_of(w_in, layer)
    in_specs[blocks + 2] = layer_of(w_down, layer)
    out = [((rows, width), BF16)] * blocks + [((rows * blocks, hidden), BF16)]
    res = pl.pallas_call(
        functools.partial(ffn_bwd_body, blocks),
        grid=(1,),
        in_specs=in_specs,
        out_specs=[whole(s) for s, _ in out],
        out_shape=[jax.ShapeDtypeStruct(s, d) for s, d in out],
        compiler_params=pltpu.CompilerParams(vmem_limit_bytes=SMALL),
        cost_estimate=pl.CostEstimate(
            flops=4 * rows * blocks * width * hidden, bytes_accessed=6_000_000, transcendentals=0
        ),
        name="ffn_bwd",
    )(*args)
    return res[:blocks], res[blocks]


def ffn_grads_body(blocks, chunks, *refs):
    n_refs, g_refs = refs[:blocks], refs[blocks : 2 * blocks]
    hid_refs, gpre_refs = refs[2 * blocks : 2 * blocks + 2], refs[2 * blocks + 2 : 2 * blocks + 4]
    out_ref = refs[-1]
    rows, width = n_refs[0].shape
    per = width // chunks
    for part, (left_refs, right_refs) in enumerate(((n_refs, gpre_refs), (g_refs, hid_refs))):
        left = jnp.concatenate([ref[...].T for ref in left_refs], 1)
        right = jnp.concatenate([ref[...] for ref in right_refs], 0)
        grad = dot_nn(left, right).astype(BF16)
        for c in range(chunks):
            place = 2 * sum(((c >> i) & 1) * (chunks >> (i + 1)) for i in range(chunks.bit_length() - 1)) + part
            out_ref[place * per : (place + 1) * per, :] = grad[c * per : (c + 1) * per]


def ffn_grads(n_blocks, g_blocks, hids, gpres, chunks):
    blocks = len(n_blocks)
    rows, width = n_blocks[0].shape
    hidden = hids[0].shape[1]
    args = (*n_blocks, *g_blocks, *hids, *gpres)
    return pl.pallas_call(
        functools.partial(ffn_grads_body, blocks, chunks),
        grid=(1,),
        in_specs=[whole(a.shape) for a in args],
        out_specs=whole((2 * width, hidden)),
        out_shape=jax.ShapeDtypeStruct((2 * width, hidden), BF16),
        compiler_params=pltpu.CompilerParams(vmem_limit_bytes=VMEM),
        cost_estimate=pl.CostEstimate(
            flops=4 * rows * blocks * width * hidden, bytes_accessed=9_000_000, transcendentals=0
        ),
        name="ffn_grads",
    )(*args)


def swap(value, axis, bit):
    size = lax.axis_size(axis)
    return lax.ppermute(value, axis, [(i, i ^ bit) for i in range(size)])


def after(values, *done):
    return lax.optimization_barrier((values, done))[0]


def gather_near(value):
    half = lax.axis_size("tp") // 2
    far = swap(value, "tp", half)
    near = [value]
    bit = 1
    while bit < half:
        near += [swap(b, "tp", bit) for b in near]
        bit *= 2
    return near, far


def gather_far(far):
    half = lax.axis_size("tp") // 2
    blocks = [far]
    bit = 1
    while bit < half:
        blocks += [swap(b, "tp", bit) for b in blocks]
        bit *= 2
    return blocks


def gather_blocks(value):
    near, far = gather_near(value)
    return near + gather_far(far)


def scatter_begin(blocks):
    blocks = list(blocks)
    bit = 1
    while bit < lax.axis_size("tp") // 2:
        size = len(blocks)
        keep = [blocks[r] for r in range(size) if not r & 1]
        sent = [swap(blocks[r], "tp", bit) for r in range(size) if r & 1]
        blocks = [a.astype(F32) + b.astype(F32) for a, b in zip(keep, sent)]
        bit *= 2
        blocks = [blocks[0]] + [b.astype(BF16) for b in blocks[1:]]
    return blocks[0].astype(F32), swap(blocks[1], "tp", bit)


def halve_begin(part, axis, bit):
    mine = (lax.axis_index(axis) // bit) & 1
    pair = part.reshape(2, part.shape[0] // 2, part.shape[1])
    sent = lax.dynamic_index_in_dim(pair, 1 - mine, 0, keepdims=False)
    kept = lax.dynamic_index_in_dim(pair, mine, 0, keepdims=False)
    return kept, swap(sent, axis, bit)


def halve_end(kept, got):
    return (kept.astype(F32) + got.astype(F32)).astype(BF16)


class Scatter:
    def __init__(self, parts, steps):
        self.steps = list(steps)
        self.begin(parts)

    def begin(self, parts):
        step = self.steps.pop(0)
        self.kept, self.got = zip(*[halve_begin(part, *step) for part in parts])

    def advance(self, *done):
        if self.steps:
            got = after(self.got, *done)
            self.begin([halve_end(a, b) for a, b in zip(self.kept, got)])

    def finish(self, *done):
        while self.steps:
            self.advance(*done)
        return [a.astype(F32) + b.astype(F32) for a, b in zip(self.kept, after(self.got, *done))]


def steps_of(axis):
    return [(axis, 1 << i) for i in range(lax.axis_size(axis).bit_length() - 1)]


HALVINGS = PIECES.bit_length() - 1


def place_of(order):
    number = 0
    for axis, bit in order[:HALVINGS]:
        number = 2 * number + ((lax.axis_index(axis) // bit) & 1)
    return number


def sum_start(part, order, stage):
    if stage < HALVINGS:
        rows = part.shape[0] // 2
        return part[:rows], swap(part[rows:], *order[stage])
    return part, swap(part, *order[stage])


def spread(part, got):
    return jnp.concatenate([part, got], 0)


class Butterfly:
    def __init__(self, value):
        self.value = value
        self.steps = steps_of("tp") + steps_of("dp")
        self.got = None

    def start(self):
        if self.steps:
            self.got = swap(self.value, *self.steps.pop(0))
            return [self.got]
        return []

    def end(self, got):
        for g in got:
            self.value = self.value + g


def on_device(
    x_in, segments, w_qkv, w_out, mix_pre, mix_post, gain_attn, gain_ffn, w_in, w_down, cotangent
):
    rows, _, width = x_in.shape
    heads = mix_pre.shape[1]
    head_size = width // heads
    tp_size = lax.axis_size("tp")
    dp_size = lax.axis_size("dp")
    tp_index = lax.axis_index("tp")
    seg = segments[:, 0]
    side = rows // 2
    span = jnp.arange(side, dtype=jnp.int32)
    starts = [chunk_of(tp_index, x, tp_size, False) * side for x in range(2)]
    qpos = jnp.concatenate([start + span for start in starts])
    qseg = jnp.concatenate([lax.dynamic_slice_in_dim(seg, start, side, 0) for start in starts])
    qinfo = jnp.stack([qpos, qseg] + [qpos] * 6, 1)
    kinfo = jnp.pad(jnp.stack([jnp.arange(seg.shape[0], dtype=jnp.int32), seg]), ((0, 6), (0, 0)))
    where = (qinfo, kinfo, tp_index[None])

    def mirror(value):
        moved = lax.ppermute(value[side:], "tp", [(i, tp_size - 1 - i) for i in range(tp_size)])
        return value[:side], moved

    tab = jnp.concatenate([jnp.swapaxes(mix_pre, 1, 2) * (head_size**-0.5), mix_post], 1)
    tabt = jnp.pad(jnp.repeat(jnp.swapaxes(tab, 1, 2), head_size, axis=1), ((0, 0), (0, 0), (0, 128 - 2 * heads)))
    tab = jnp.repeat(tab, head_size, axis=2)

    stream = x_in[:, 0].astype(F32)
    x_folded = jnp.concatenate(mirror(x_in[:, 0]), 0).astype(F32)
    kept = []
    half = tp_size // 2
    for layer in range(LAYERS):
        last = layer == LAYERS - 1
        n1_blocks = gather_blocks(rms(stream, gain_attn[layer]).astype(BF16))
        if last:
            low, n1_blocks[half] = after((cotangent[:, 0], n1_blocks[half]))
            grad_near, grad_far = gather_near(low)
        else:
            stream = x_folded
        p, u, q, k, v, ot, n1t, middle, n2 = attn_fwd(
            layer,
            layer == 0,
            n1_blocks,
            stream,
            w_qkv,
            w_out,
            tab,
            gain_ffn,
            where,
        )
        if last:
            n2, grad_near, grad_far = after((n2, grad_near, grad_far))
        near, far = gather_near(n2)
        out_a, hid_a, dgelu_a = ffn_fwd(layer, near, w_in, w_down)
        if last:
            given = grad_near + gather_far(grad_far)
            gf_blocks = [jnp.concatenate([given[r][:side], given[tp_size - 1 - r][side:]], 0) for r in range(tp_size)]
            gn2_a, gpre_a = ffn_bwd(layer, gf_blocks[:half], dgelu_a, w_in, w_down)
            far, gpre_a = after((far, gpre_a))
        far, hid_a = after((far, hid_a))
        n2_blocks = near + gather_far(far)
        out_b, hid_b, dgelu_b = ffn_fwd(layer, n2_blocks[half:], w_in, w_down)
        kept.append((stream, n1t, p, u, q, k, v, ot, middle, n2_blocks, hid_a, hid_b, dgelu_a, dgelu_b))
        if not last:
            own, far = scatter_begin([*out_a, *out_b])
            stream = middle + (own + far.astype(F32))

    grad_flow = gf_blocks[0].astype(F32)
    per = width // dp_size
    small = [None] * LAYERS
    sharded = [None] * LAYERS
    for layer in range(LAYERS - 1, -1, -1):
        last = layer == LAYERS - 1
        stream, n1t, p, u, q, k, v, ot, middle, n2_blocks, hid_a, hid_b, dgelu_a, dgelu_b = kept[layer]
        if not last:
            near, far = gather_near(grad_flow.astype(BF16))
            gn2_a, gpre_a = ffn_bwd(layer, near, dgelu_a, w_in, w_down)
            far, gpre_a = after((far, gpre_a))
            gf_blocks = near + gather_far(far)
        gn2_b, gpre_b = ffn_bwd(layer, gf_blocks[half:], dgelu_b, w_in, w_down)
        if not last:
            total_got, gpre_b = after((total_got, gpre_b))
            total = halve_end(total_kept, total_got)
            total_kept, total_got = sum_start(total, total_order, 1)
        own, far = scatter_begin([*gn2_a, *gn2_b])
        packed = ffn_grads(n2_blocks, gf_blocks, (hid_a, hid_b), (gpre_a, gpre_b), dp_size)
        far, packed = after((far, packed))
        if not last:
            total_got, packed = after((total_got, packed))
            total = halve_end(total_kept, total_got)
            total_kept, total_got = sum_start(total, total_order, 2)
        if not last:
            previous = moving
        moving = Scatter([packed], steps_of("dp"))
        gn2 = (own + far.astype(F32)).astype(BF16).astype(F32)
        grad_norm, grad_gffn = rms_back(gn2, middle, gain_ffn[layer])
        grad_middle = grad_flow + grad_norm
        ga = grad_middle.astype(BF16)
        if last:
            orders = [steps_of("dp") + steps_of("tp")[1:]]
        else:
            (y_step, *dp_rest), x_steps = steps_of("dp"), steps_of("tp")[1:]
            orders = [x_steps + [y_step] + dp_rest, [y_step] + x_steps + dp_rest]
        place = jnp.stack([tp_index & 1] + [place_of(order) for order in orders] + [tp_index])
        parts, grads, zpre, zpost = attn_bwd(
            layer, tp_size, ga, w_out, q, k, v, p, u, tab, tabt, place, w_qkv, n1t, ot
        )
        core_step = steps_of("tp")[0]
        if last:
            parts, grads, moving.got = after((parts, grads, moving.got))
            y_middle = middle
            keep, send = grads
            total = halve_end(keep, swap(send, *core_step))
            own, far = scatter_begin(parts)
            moving.advance()
            far, moving.got = after((far, moving.got), total)
            moving.advance()
            (total_order,), total_place = orders, place
            total_kept, total_got = sum_start(total, total_order, 0)
        else:
            parts, grads, moving.got, total_got, previous.got = after(
                (parts, grads, moving.got, total_got, previous.got)
            )
            (summed,) = previous.finish()
            sharded[layer + 1] = (summed[:per], summed[per:].T)
        if not last:
            break
        gn1 = (own + far.astype(F32)).astype(BF16).astype(F32)
        grad_norm, grad_gattn = rms_back(gn1, stream, gain_attn[layer])
        grad_flow = grad_middle + grad_norm
        grad_mpre = jnp.sum(zpre.reshape(heads, heads, head_size), -1).T * (head_size**-0.5)
        grad_mpost = jnp.sum(zpost.reshape(heads, heads, head_size), -1)
        small[layer] = (grad_mpre, grad_mpost, grad_gattn, grad_gffn)

    total = halve_end(total_kept, total_got)
    got = [swap(send, *core_step) for send in grads[1::2]]
    pieces = [halve_end(keep, g) for keep, g in zip(grads[::2], got)]
    for stage in range(HALVINGS, len(total_order)):
        total_got = swap(total, *total_order[stage])
        pieces, total_got = after((pieces, total_got))
        total = halve_end(total, total_got)
    own, far = scatter_begin(parts)
    for stage in range(HALVINGS):
        kept, got = zip(*[sum_start(part, order, stage) for part, order in zip(pieces, orders)])
        total_got = swap(total, *total_order[HALVINGS - 1 - stage])
        if stage < HALVINGS - 1:
            got, total_got = after((got, total_got))
            total = spread(total, total_got)
        if stage == HALVINGS - 1:
            flat_got = flat.start()
            got, flat_got = after((got, flat_got))
            flat.end(flat_got)
        pieces = [halve_end(a, b) for a, b in zip(kept, after(got))]
        if stage == 0:
            far, pieces = after((far, pieces))
            gn1 = (own + far.astype(F32)).astype(BF16).astype(F32)
            grad_norm, grad_gattn = rms_back(gn1, stream, gain_attn[layer])
            grad_flow = grad_middle + grad_norm
            grad_mpre = jnp.sum(zpre.reshape(heads, heads, head_size), -1).T * (head_size**-0.5)
            grad_mpost = jnp.sum(zpost.reshape(heads, heads, head_size), -1)
            small[layer] = (grad_mpre, grad_mpost, grad_gattn, grad_gffn)
            mixes = jnp.concatenate([a.reshape(-1) for s in small for a in s[:2]])
            count = mixes.shape[0]
            mix_rows = -(-count // width)
            flat = jnp.concatenate(
                [jnp.pad(mixes, (0, mix_rows * width - count)).reshape(mix_rows, width)]
                + [g[None] for s in small for g in s[2:]]
            )
            flat = jnp.pad(flat, ((0, -flat.shape[0] % 8), (0, 0)))
            flat = Butterfly(flat)
        if stage == 1:
            moving.advance(*pieces)
            y_parts, pieces = after(([*out_a, *out_b], pieces))
            own_y, far_y = scatter_begin(y_parts)
    for stage in range(HALVINGS, len(orders[0])):
        got = [swap(part, *order[stage]) for part, order in zip(pieces, orders)]
        flat_got = flat.start()
        if stage == HALVINGS:
            first_rows, second_rows = mirror(grad_flow)
            got, second_rows, total_got, moving.got, far_y = after((got, second_rows, total_got, moving.got, far_y))
            y_out = (y_middle + (own_y + far_y.astype(F32))).astype(BF16)
            y_first, y_second = mirror(y_out)
            grad_x = jnp.concatenate([first_rows, second_rows], 0)
            total = spread(total, total_got)
            moving.advance()
        got, flat_got = after((got, flat_got))
        flat.end(flat_got)
        pieces = [halve_end(a, b) for a, b in zip(pieces, got)]
    total_other = swap(total, *core_step)
    replicated = ()
    for stage in range(HALVINGS - 1, -1, -1):
        got = [swap(part, *order[stage]) for part, order in zip(pieces, orders)]
        flat_got = flat.start()
        if stage == HALVINGS - 1:
            got, total_other = after((got, total_other))
        elif stage == HALVINGS - 2:
            replicated = expand(1, 0, total_place, [total])
            got, replicated, moving.got, y_second = after((got, replicated, moving.got, y_second))
            y_out = jnp.concatenate([y_first, y_second], 0)
        elif stage == 0:
            replicated = expand(1, 1, total_place, [total_other], replicated)
            got, replicated = after((got, replicated))
        got, flat_got = after((got, flat_got))
        flat.end(flat_got)
        pieces = [spread(a, b) for a, b in zip(pieces, got)]
    got = [swap(part, *core_step) for part in pieces]
    while flat.steps:
        flat.end(flat.start())
    flat = flat.value
    (summed,) = moving.finish()
    sharded[0] = (summed[:per], summed[per:].T)
    replicated = expand(0, 0, place, pieces, replicated)
    got, replicated, sharded = after((got, replicated, sharded))
    replicated = expand(0, 1, place, got, replicated)
    mixes = flat[:mix_rows].reshape(-1)[:count].reshape(LAYERS, 2, heads, heads)
    gains = flat[mix_rows : mix_rows + 2 * LAYERS].reshape(LAYERS, 2, width)
    return (
        y_out[:, None],
        grad_x[:, None],
        *replicated,
        mixes[:, 0],
        mixes[:, 1],
        gains[:, 0],
        gains[:, 1],
        jnp.stack([s[0] for s in sharded]),
        jnp.stack([s[1] for s in sharded]),
    )


def solution(mesh):
    in_specs = (
        P("tp", "dp", None),
        P(None, "dp"),
        P(),
        P(),
        P(),
        P(),
        P(),
        P(),
        P(None, None, "tp"),
        P(None, "tp", None),
        P("tp", "dp", None),
    )
    out_specs = (
        P("tp", "dp", None),
        P("tp", "dp", None),
        P(),
        P(),
        P(),
        P(),
        P(),
        P(),
        P(None, "dp", "tp"),
        P(None, "tp", "dp"),
    )
    return jax.shard_map(
        on_device, mesh=mesh, in_specs=in_specs, out_specs=out_specs, check_vma=False
    )
```

profile of v0, /device:TPU:0, one launch (start us, length us, event | category | flops | bytes accessed | tf_op | source)
XLA Modules:
  0.0 451.3 jit_solution(13621543459696238579)
XLA Ops:
  7.2 9.6 %collective-permute-done.1.refs_2_ = bf16[256,768]{1,0:T(8,128)(2,1)S(1)} collective-permute-done((bf16[256,768]{1,0:T(8,128)(2,1)S(1)}, bf16[256,768]{1,0:T(8,128)(2,1)S(1)}, u32[]{:S(2)}, u32[]{:S(2)}) %collective-permute-start.1) | collective-permute-done | bytes 393248 | tf_op jit(solution)/shard_map/ppermute | solution.py:545
  26.8 20.9 %attn_fwd.2 = (bf16[12,256,1024]{2,1,0:T(8,128)(2,1)}, bf16[12,256,768]{2,1,0:T(8,128)(2,1)}, bf16[256,768]{1,0:T(8,128)(2,1)S(1)}, bf16[1024,768]{1,0:T(8,128)(...) custom-call(bf16[256,768]{1,0:T(8,128)(2,1)S(1)} %fusion.30.refs_0_,, ...), custom_call_target="tpu_custom_call" | custom-call | flops 9663676416 | bytes 20000000 | tf_op jit(solution)/shard_map/attn_fwd/pallas_call | solution.py:184
  54.4 6.1 %collective-permute-done.6.refs_0_.refs_2_ = bf16[256,768]{1,0:T(8,128)(2,1)S(1)} collective-permute-done((bf16[256,768]{1,0:T(8,128)(2,1)S(1)}, bf16[256,768]{1,0:T(8,128)(2,1)S(1)}, u32[]{:S(2)}, u32[]{:S(2)}) %collective-permute-start.6) | collective-permute-done | bytes 393248 | tf_op jit(solution)/shard_map/ppermute | solution.py:545
  67.3 9.8 %collective-permute-done.9 = bf16[256,768]{1,0:T(8,128)(2,1)S(1)} collective-permute-done((bf16[256,768]{1,0:T(8,128)(2,1)S(1)}, bf16[256,768]{1,0:T(8,128)(2,1)S(1)}, u32[]{:S(2)}, u32[]{:S(2)}) %collective-permute-start.9) | collective-permute-done | bytes 393248 | tf_op jit(solution)/shard_map/ppermute | solution.py:545
  79.6 8.9 %collective-permute-done.11.refs_2_ = bf16[256,768]{1,0:T(8,128)(2,1)S(1)} collective-permute-done((bf16[256,768]{1,0:T(8,128)(2,1)S(1)}, bf16[256,768]{1,0:T(8,128)(2,1)S(1)}, u32[]{:S(2)}, u32[]{:S(2)}) %collective-permute-start.11) | collective-permute-done | bytes 393248 | tf_op jit(solution)/shard_map/ppermute | solution.py:545
  90.4 21.0 %attn_fwd.3 = (bf16[12,256,1024]{2,1,0:T(8,128)(2,1)}, bf16[12,256,768]{2,1,0:T(8,128)(2,1)}, bf16[256,768]{1,0:T(8,128)(2,1)S(1)}, bf16[1024,768]{1,0:T(8,128)(...) custom-call(bf16[256,768]{1,0:T(8,128)(2,1)S(1)} %multiply_convert_f, ...), custom_call_target="tpu_custom_call" | custom-call | flops 9663676416 | bytes 20000000 | tf_op jit(solution)/shard_map/attn_fwd/pallas_call | solution.py:184
  143.3 6.9 %ffn_grads.2 = bf16[1536,768]{1,0:T(8,128)(2,1)} custom-call(bf16[256,768]{1,0:T(8,128)(2,1)} %copy-done.34, bf16[256,768]{1,0:T(8,128)(2,1)} %copy-done.35, bf16[256,768]{1,0:T(8,128)(2,1)} %copy-done.36, bf16[256,768]{1,0:T(8,128)(2,1)} %copy-done.37, bf16[256,768]{1,0:T(8,128)(2,1)} %copy-done.10, bf16[256,768]{1,0:T(8,128)(2,1)} %copy-done.9, ...), custom_call_target="tpu_custom_call" | custom-call | flops 2415919104 | bytes 9000000 | tf_op jit(solution)/shard_map/ffn_grads/pallas_call | solution.py:529
  150.1 3.7 collective-permute-done.21
  160.1 32.2 %attn_bwd.2 = (bf16[256,768]{1,0:T(8,128)(2,1)}, bf16[256,768]{1,0:T(8,128)(2,1)}, bf16[256,768]{1,0:T(8,128)(2,1)}, bf16[256,768]{1,0:T(8,128)(2,1)}, bf16[384,...) custom-call(bf16[256,768]{1,0:T(8,128)(2,1)} %get-tuple-element.419.refs_0_, ...), custom_call_target="tpu_custom_call" | custom-call | flops 38654705664 | bytes 20000000 | tf_op jit(solution)/shard_map/attn_bwd/pallas_call | solution.py:348
  200.4 9.9 %collective-permute-done.26 = bf16[384,768]{1,0:T(8,128)(2,1)S(1)} collective-permute-done((bf16[384,768]{1,0:T(8,128)(2,1)S(1)}, bf16[384,768]{1,0:T(8,128)(2,1)S(1)}, u32[]{:S(2)}, u32[]{:S(2)}) %collective-permute-start.26) | collective-permute-done | bytes 589856 | tf_op jit(solution)/shard_map/ppermute | solution.py:545
  218.4 5.3 %collective-permute-done.30.refs_0_.refs_6_ = bf16[256,768]{1,0:T(8,128)(2,1)} collective-permute-done((bf16[256,768]{1,0:T(8,128)(2,1)S(1)}, bf16[256,768]{1,0:T(8,128)(2,1)}, u32[]{:S(2)}, u32[]{:S(2)}) %collective-permute-start.30) | collective-permute-done | bytes 393248 | tf_op jit(solution)/shard_map/ppermute | solution.py:545
  235.3 6.7 %collective-permute-done.34 = bf16[192,3072]{1,0:T(8,128)(2,1)} collective-permute-done((bf16[192,3072]{1,0:T(8,128)(2,1)}, bf16[192,3072]{1,0:T(8,128)(2,1)}, u32[]{:S(2)}, u32[]{:S(2)}) %collective-permute-start.34) | collective-permute-done | bytes 1179680 | tf_op jit(solution)/shard_map/ppermute | solution.py:545
  248.0 7.0 %ffn_grads.3 = bf16[1536,768]{1,0:T(8,128)(2,1)} custom-call(bf16[256,768]{1,0:T(8,128)(2,1)} %copy-done.30, bf16[256,768]{1,0:T(8,128)(2,1)} %copy-done.31, bf16[256,768]{1,0:T(8,128)(2,1)} %copy-done.32, bf16[256,768]{1,0:T(8,128)(2,1)} %copy-done.33, bf16[256,768]{1,0:T(8,128)(2,1)} %copy-done.13, bf16[256,768]{1,0:T(8,128)(2,1)} %copy-done.20, ...), custom_call_target="tpu_custom_call" | custom-call | flops 2415919104 | bytes 9000000 | tf_op jit(solution)/shard_map/ffn_grads/pallas_call | solution.py:529
  258.8 3.2 collective-permute-done.35
  265.6 32.1 %attn_bwd.3 = (bf16[256,768]{1,0:T(8,128)(2,1)}, bf16[256,768]{1,0:T(8,128)(2,1)}, bf16[256,768]{1,0:T(8,128)(2,1)}, bf16[256,768]{1,0:T(8,128)(2,1)}, bf16[384,...) custom-call(bf16[256,768]{1,0:T(8,128)(2,1)} %get-tuple-element.415., ...), custom_call_target="tpu_custom_call" | custom-call | flops 38654705664 | bytes 20000000 | tf_op jit(solution)/shard_map/attn_bwd/pallas_call | solution.py:348
  306.0 6.0 %collective-permute-done.43 = bf16[48,3072]{1,0:T(8,128)(2,1)S(1)} collective-permute-done((bf16[48,3072]{1,0:T(8,128)(2,1)S(1)}, bf16[48,3072]{1,0:T(8,128)(2,1)S(1)}, u32[]{:S(2)}, u32[]{:S(2)}) %collective-permute-start.43) | collective-permute-done | bytes 294944 | tf_op jit(solution)/shard_map/ppermute | solution.py:545
  318.7 11.0 %collective-permute-done.46 = bf16[48,3072]{1,0:T(8,128)(2,1)S(1)} collective-permute-done((bf16[48,3072]{1,0:T(8,128)(2,1)S(1)}, bf16[48,3072]{1,0:T(8,128)(2,1)S(1)}, u32[]{:S(2)}, u32[]{:S(2)}) %collective-permute-start.46) | collective-permute-done | bytes 294944 | tf_op jit(solution)/shard_map/ppermute | solution.py:545
  330.0 5.5 %collective-permute-done.40 = bf16[256,768]{1,0:T(8,128)(2,1)S(1)} collective-permute-done((bf16[256,768]{1,0:T(8,128)(2,1)S(1)}, bf16[256,768]{1,0:T(8,128)(2,1)S(1)}, u32[]{:S(2)}, u32[]{:S(2)}) %collective-permute-start.40) | collective-permute-done | bytes 393248 | tf_op jit(solution)/shard_map/ppermute | solution.py:545
  350.9 3.4 collective-permute-done.49
  370.3 9.6 %collective-permute-done.55 = bf16[48,1536]{1,0:T(8,128)(2,1)S(1)} collective-permute-done((bf16[48,1536]{1,0:T(8,128)(2,1)S(1)}, bf16[48,1536]{1,0:T(8,128)(2,1)S(1)}, u32[]{:S(2)}, u32[]{:S(2)}) %collective-permute-start.55) | collective-permute-done | bytes 147488 | tf_op jit(solution)/shard_map/ppermute | solution.py:545
  393.0 4.0 collective-permute-done.63
  405.3 4.2 collective-permute-done.70
  419.8 7.0 %collective-permute-done.72 = bf16[192,1536]{1,0:T(8,128)(2,1)} collective-permute-done((bf16[192,1536]{1,0:T(8,128)(2,1)}, bf16[192,1536]{1,0:T(8,128)(2,1)}, u32[]{:S(2)}, u32[]{:S(2)}) %collective-permute-start.72) | collective-permute-done | bytes 589856 | tf_op jit(solution)/shard_map/ppermute | solution.py:545
  446.2 4.7 %expand.7 = (f32[2,768,2304]{2,1,0:T(8,128)}, f32[2,768,768]{2,1,0:T(8,128)}) custom-call(s32[4]{0:T(128)S(1)} %copy-done.40, bf16[384,1536]{1,0:T(8,128)(2,1)S(1)} %collective-permute-done.75.refs_0_, bf16[384,1536]{1,0:T(8,128)(2,1)} %collective-permute-done.76.refs_1_, ...), custom_call_target="tpu_custom_call", output_to_operand_aliasing={{0}: (3, {}), {1}: (4, {})} | custom-call | bytes 7000000 | tf_op jit(solution)/shard_map/expand/pallas_call | solution.py:411
  (605 shorter events, 209.7 us)
Async XLA Ops:
  3.8 16.8 %collective-permute-start = (bf16[256,768]{1,0:T(8,128)(2,1)S(1)}, bf16[256,768]{1,0:T(8,128)(2,1)S(1)}, u32[]{:S(2)}, u32[]{:S(2)}) collective-permute-start(bf16[256,768]{1,0:T(8,128)(2,1)S(1)} %fusion.30.refs_0_), channel_id=1, source_target_pairs={{0,1},{1,0},{2,3},{3,2},{4,5},{5,4},{6,7},{7,6},{8,9},{9,8},{10,11... | collective-permute-start | bytes 1179656 | tf_op jit(solution)/shard_map/ppermute | solution.py:545
  88.5 26.5 %collective-permute-start.13 = (bf16[256,768]{1,0:T(8,128)(2,1)S(1)}, bf16[256,768]{1,0:T(8,128)(2,1)S(1)}, u32[]{:S(2)}, u32[]{:S(2)}) collective-permute-start(bf16[256,768]{1,0:T(8,128)(2,1)S(1)} %bitcast.105), channel_id=1, source_target_pairs={{0,1},{1,0},{2,3},{3,2},{4,5},{5,4},{6,7},{7,6},{8,9},{9,8},{10,11... | collective-permute-start | bytes 1179656 | tf_op jit(solution)/shard_map/ppermute | solution.py:545
  89.0 26.0 %collective-permute-start.14 = (bf16[256,768]{1,0:T(8,128)(2,1)S(1)}, bf16[256,768]{1,0:T(8,128)(2,1)S(1)}, u32[]{:S(2)}, u32[]{:S(2)}) collective-permute-start(bf16[256,768]{1,0:T(8,128)(2,1)S(1)} %bitcast.106), channel_id=1, source_target_pairs={{0,2},{1,3},{2,0},{3,1},{4,6},{5,7},{6,4},{7,5},{8,10},{9,11},{10,... | collective-permute-start | bytes 1179656 | tf_op jit(solution)/shard_map/ppermute | solution.py:545
  157.3 35.0 %collective-permute-start.22 = (bf16[768,768]{1,0:T(8,128)(2,1)}, bf16[768,768]{1,0:T(8,128)(2,1)}, u32[]{:S(2)}, u32[]{:S(2)}) collective-permute-start(bf16[768,768]{1,0:T(8,128)(2,1)} %dynamic-slice_bitcast_fusion.1), channel_id=1, source_target_pairs={{0,4},{4,0},{8,12},{12,8},{16,20},{20,16},{24,28},{28,24},{1,5},{5... | collective-permute-start | bytes 3538952 | tf_op jit(solution)/shard_map/ppermute | solution.py:545
  195.0 15.4 %collective-permute-start.26 = (bf16[384,768]{1,0:T(8,128)(2,1)S(1)}, bf16[384,768]{1,0:T(8,128)(2,1)S(1)}, u32[]{:S(2)}, u32[]{:S(2)}) collective-permute-start(bf16[384,768]{1,0:T(8,128)(2,1)S(1)} %dynamic-slice_bitcast_fusion.3), channel_id=1, source_target_pairs={{0,8},{4,12},{8,0},{12,4},{16,24},{20,28},{24,16},{28,20},{1,9},{5... | collective-permute-start | bytes 1769480 | tf_op jit(solution)/shard_map/ppermute | solution.py:545
  213.4 28.6 %collective-permute-start.34 = (bf16[192,3072]{1,0:T(8,128)(2,1)}, bf16[192,3072]{1,0:T(8,128)(2,1)}, u32[]{:S(2)}, u32[]{:S(2)}) collective-permute-start(bf16[192,3072]{1,0:T(8,128)(2,1)} %slice.199), channel_id=1, source_target_pairs={{0,4},{4,0},{8,12},{12,8},{16,20},{20,16},{24,28},{28,24},{1,5},{5... | collective-permute-start | bytes 3538952 | tf_op jit(solution)/shard_map/ppermute | solution.py:545
  232.7 65.0 %collective-permute-start.38 = (bf16[192,768]{1,0:T(8,128)(2,1)}, bf16[192,768]{1,0:T(8,128)(2,1)}, u32[]{:S(2)}, u32[]{:S(2)}) collective-permute-start(bf16[192,768]{1,0:T(8,128)(2,1)} %dynamic-slice_bitcast_fusion.5), channel_id=1, source_target_pairs={{0,16},{4,20},{8,24},{12,28},{16,0},{20,4},{24,8},{28,12},{1,17},{... | collective-permute-start | bytes 884744 | tf_op jit(solution)/shard_map/ppermute | solution.py:545
  235.3 19.7 %collective-permute-start.29 = (bf16[256,768]{1,0:T(8,128)(2,1)S(1)}, bf16[256,768]{1,0:T(8,128)(2,1)}, u32[]{:S(2)}, u32[]{:S(2)}) collective-permute-start(bf16[256,768]{1,0:T(8,128)(2,1)S(1)} %copy-done.58), channel_id=1, source_target_pairs={{0,1},{1,0},{2,3},{3,2},{4,5},{5,4},{6,7},{7,6},{8,9},{9,8},{10,11... | collective-permute-start | bytes 1179656 | tf_op jit(solution)/shard_map/ppermute | solution.py:545
  246.4 15.5 %collective-permute-start.35 = (bf16[96,3072]{1,0:T(8,128)(2,1)}, bf16[96,3072]{1,0:T(8,128)(2,1)}, u32[]{:S(2)}, u32[]{:S(2)}) collective-permute-start(bf16[96,3072]{1,0:T(8,128)(2,1)} %slice.201), channel_id=1, source_target_pairs={{0,8},{4,12},{8,0},{12,4},{16,24},{20,28},{24,16},{28,20},{1,9},{5... | collective-permute-start | bytes 1769480 | tf_op jit(solution)/shard_map/ppermute | solution.py:545
  262.0 35.7 %collective-permute-start.36 = (bf16[768,768]{1,0:T(8,128)(2,1)S(1)}, bf16[768,768]{1,0:T(8,128)(2,1)}, u32[]{:S(2)}, u32[]{:S(2)}) collective-permute-start(bf16[768,768]{1,0:T(8,128)(2,1)S(1)} %dynamic-slice_bitcast_fusion), channel_id=1, source_target_pairs={{0,4},{4,0},{8,12},{12,8},{16,20},{20,16},{24,28},{28,24},{1,5},{5... | collective-permute-start | bytes 3538952 | tf_op jit(solution)/shard_map/ppermute | solution.py:545
  263.8 33.9 %collective-permute-start.37 = (bf16[48,3072]{1,0:T(8,128)(2,1)S(1)}, bf16[48,3072]{1,0:T(8,128)(2,1)S(1)}, u32[]{:S(2)}, u32[]{:S(2)}) collective-permute-start(bf16[48,3072]{1,0:T(8,128)(2,1)S(1)} %slice.203), channel_id=1, source_target_pairs={{0,16},{4,20},{8,24},{12,28},{16,0},{20,4},{24,8},{28,12},{1,17},{... | collective-permute-start | bytes 884744 | tf_op jit(solution)/shard_map/ppermute | solution.py:545
  312.1 17.5 %collective-permute-start.44 = (bf16[192,1536]{1,0:T(8,128)(2,1)S(1)}, bf16[192,1536]{1,0:T(8,128)(2,1)S(1)}, u32[]{:S(2)}, u32[]{:S(2)}) collective-permute-start(bf16[192,1536]{1,0:T(8,128)(2,1)S(1)} %slice.172), channel_id=1, source_target_pairs={{0,2},{1,3},{2,0},{3,1},{4,6},{5,7},{6,4},{7,5},{8,10},{9,11},{10,... | collective-permute-start | bytes 1769480 | tf_op jit(solution)/shard_map/ppermute | solution.py:545
  312.5 17.2 %collective-permute-start.45 = (bf16[192,1536]{1,0:T(8,128)(2,1)S(1)}, bf16[192,1536]{1,0:T(8,128)(2,1)S(1)}, u32[]{:S(2)}, u32[]{:S(2)}) collective-permute-start(bf16[192,1536]{1,0:T(8,128)(2,1)S(1)} %slice.173), channel_id=1, source_target_pairs={{0,4},{4,0},{8,12},{12,8},{16,20},{20,16},{24,28},{28,24},{1,5},{5... | collective-permute-start | bytes 1769480 | tf_op jit(solution)/shard_map/ppermute | solution.py:545
  314.2 15.5 %collective-permute-start.46 = (bf16[48,3072]{1,0:T(8,128)(2,1)S(1)}, bf16[48,3072]{1,0:T(8,128)(2,1)S(1)}, u32[]{:S(2)}, u32[]{:S(2)}) collective-permute-start(bf16[48,3072]{1,0:T(8,128)(2,1)S(1)} %add_convert_fusion.20), channel_id=1, source_target_pairs={{0,16},{4,20},{8,24},{12,28},{16,0},{20,4},{24,8},{28,12},{1,17},{... | collective-permute-start | bytes 884744 | tf_op jit(solution)/shard_map/ppermute | solution.py:545
  316.7 25.5 %collective-permute-start.53 = (bf16[256,768]{1,0:T(8,128)(2,1)S(1)}, bf16[256,768]{1,0:T(8,128)(2,1)S(1)}, u32[]{:S(2)}, u32[]{:S(2)}) collective-permute-start(bf16[256,768]{1,0:T(8,128)(2,1)S(1)} %copy-done.149), channel_id=1, source_target_pairs={{0,1},{1,0},{2,3},{3,2},{4,5},{5,4},{6,7},{7,6},{8,9},{9,8},{10,11... | collective-permute-start | bytes 1179656 | tf_op jit(solution)/shard_map/ppermute | solution.py:545
  316.9 18.6 %collective-permute-start.40 = (bf16[256,768]{1,0:T(8,128)(2,1)S(1)}, bf16[256,768]{1,0:T(8,128)(2,1)S(1)}, u32[]{:S(2)}, u32[]{:S(2)}) collective-permute-start(bf16[256,768]{1,0:T(8,128)(2,1)S(1)} %add_convert_fusion.10), channel_id=1, source_target_pairs={{0,2},{1,3},{2,0},{3,1},{4,6},{5,7},{6,4},{7,5},{8,10},{9,11},{10,... | collective-permute-start | bytes 1179656 | tf_op jit(solution)/shard_map/ppermute | solution.py:545
  349.2 18.8 %collective-permute-start.57 = (f32[128,768]{1,0:T(8,128)S(1)}, f32[128,768]{1,0:T(8,128)S(1)}, u32[]{:S(2)}, u32[]{:S(2)}) collective-permute-start(f32[128,768]{1,0:T(8,128)S(1)} %get-tuple-element.425), channel_id=1, source_target_pairs={{0,3},{1,2},{2,1},{3,0},{4,7},{5,6},{6,5},{7,4},{8,11},{9,10},{10,... | collective-permute-start | bytes 1179656 | tf_op jit(solution)/shard_map/ppermute | solution.py:685
  358.7 25.2 %collective-permute-start.58 = (bf16[192,3072]{1,0:T(8,128)(2,1)S(1)}, bf16[192,3072]{1,0:T(8,128)(2,1)S(1)}, u32[]{:S(2)}, u32[]{:S(2)}) collective-permute-start(bf16[192,3072]{1,0:T(8,128)(2,1)S(1)} %pad_maximum_fusion.1), channel_id=1, source_target_pairs={{0,4},{4,0},{8,12},{12,8},{16,20},{20,16},{24,28},{28,24},{1,5},{5... | collective-permute-start | bytes 3538952 | tf_op jit(solution)/shard_map/ppermute | solution.py:545
  361.6 20.6 %collective-permute-start.59 = (bf16[384,768]{1,0:T(8,128)(2,1)S(1)}, bf16[384,768]{1,0:T(8,128)(2,1)S(1)}, u32[]{:S(2)}, u32[]{:S(2)}) collective-permute-start(bf16[384,768]{1,0:T(8,128)(2,1)S(1)} %dynamic-slice_bitcast_fusion.2), channel_id=1, source_target_pairs={{0,8},{4,12},{8,0},{12,4},{16,24},{20,28},{24,16},{28,20},{1,9},{5... | collective-permute-start | bytes 1769480 | tf_op jit(solution)/shard_map/ppermute | solution.py:545
  366.4 15.8 %collective-permute-start.61 = (bf16[256,768]{1,0:T(8,128)(2,1)S(1)}, bf16[256,768]{1,0:T(8,128)(2,1)S(1)}, u32[]{:S(2)}, u32[]{:S(2)}) collective-permute-start(bf16[256,768]{1,0:T(8,128)(2,1)S(1)} %add_convert_fusion.8), channel_id=1, source_target_pairs={{0,2},{1,3},{2,0},{3,1},{4,6},{5,7},{6,4},{7,5},{8,10},{9,11},{10,... | collective-permute-start | bytes 1179656 | tf_op jit(solution)/shard_map/ppermute | solution.py:545
  384.0 15.4 %collective-permute-start.65 = (bf16[384,3072]{1,0:T(8,128)(2,1)S(1)}, bf16[384,3072]{1,0:T(8,128)(2,1)S(1)}, u32[]{:S(2)}, u32[]{:S(2)}) collective-permute-start(bf16[384,3072]{1,0:T(8,128)(2,1)S(1)} %pad_maximum_fusion.refs_0_), channel_id=1, source_target_pairs={{0,1},{1,0},{2,3},{3,2},{4,5},{5,4},{6,7},{7,6},{8,9},{9,8},{10,11... | collective-permute-start | bytes 7077896 | tf_op jit(solution)/shard_map/ppermute | solution.py:545
  391.8 17.6 %collective-permute-start.69 = (bf16[192,768]{1,0:T(8,128)(2,1)S(1)}, bf16[192,768]{1,0:T(8,128)(2,1)S(1)}, u32[]{:S(2)}, u32[]{:S(2)}) collective-permute-start(bf16[192,768]{1,0:T(8,128)(2,1)S(1)} %dynamic-slice_bitcast_fusion.4), channel_id=1, source_target_pairs={{0,16},{4,20},{8,24},{12,28},{16,0},{20,4},{24,8},{28,12},{1,17},{... | collective-permute-start | bytes 884744 | tf_op jit(solution)/shard_map/ppermute | solution.py:545
  410.3 16.5 %collective-permute-start.72 = (bf16[192,1536]{1,0:T(8,128)(2,1)}, bf16[192,1536]{1,0:T(8,128)(2,1)}, u32[]{:S(2)}, u32[]{:S(2)}) collective-permute-start(bf16[192,1536]{1,0:T(8,128)(2,1)} %pad_maximum_fusion.5), channel_id=1, source_target_pairs={{0,2},{1,3},{2,0},{3,1},{4,6},{5,7},{6,4},{7,5},{8,10},{9,11},{10,... | collective-permute-start | bytes 1769480 | tf_op jit(solution)/shard_map/ppermute | solution.py:545
  411.9 16.0 %collective-permute-start.73 = (bf16[192,1536]{1,0:T(8,128)(2,1)}, bf16[192,1536]{1,0:T(8,128)(2,1)}, u32[]{:S(2)}, u32[]{:S(2)}) collective-permute-start(bf16[192,1536]{1,0:T(8,128)(2,1)} %pad_maximum_fusion.6), channel_id=1, source_target_pairs={{0,4},{4,0},{8,12},{12,8},{16,20},{20,16},{24,28},{28,24},{1,5},{5... | collective-permute-start | bytes 1769480 | tf_op jit(solution)/shard_map/ppermute | solution.py:545
  (204 other events, 1365.7 us)
where the time goes:
time: 460 us; the launch traced here: 451 us
  Pallas kernels  149 us (32%)
  waiting for transfers between devices  143 us (31%)
  starting transfers between devices  58.1 us (13%)
  local copies, waits for them, and re-layouts  54.9 us (12%)
  other arithmetic  44.2 us (10%)
    ppermute x74, waiting for transfers between devices, swap(): return lax.ppermute(value, axis, [(i, i ^ bit) for i in range(size)])  135 us
    pallas_call x2, Pallas kernels, attn_bwd(): pl.pallas_call(functools.partial(attn_bwd_body, heads, blocks, layer, par...  64.3 us
    ppermute x74, starting transfers between devices, swap(): return lax.ppermute(value, axis, [(i, i ^ bit) for i in range(size)])  56.3 us
    pallas_call x2, Pallas kernels, attn_fwd(): pl.pallas_call(functools.partial(attn_fwd_body, blocks, heads, layer, pla...  41.9 us
    unnamed x308, local copies, waits for them, and re-layouts  31.8 us
    pallas_call x4, Pallas kernels, expand(): pl.pallas_call(functools.partial(expand_body, len(halves)), grid_spec=plt...  14 us
    pallas_call x2, Pallas kernels, ffn_grads(): pl.pallas_call(functools.partial(ffn_grads_body, blocks, chunks), grid=(1...  13.9 us
    convert_element_type x19, other arithmetic, halve_end(): return (kept.astype(F32) + got.astype(F32)).astype(BF16)  12.5 us
  transfers between devices with their start and end apart: 77, of which 34 were waited for; matrix products, arithmetic and copies ran while one was open for 13% of the time, Pallas kernels for 26%

commit v1 on v0

--- a/solution.py
+++ b/solution.py
@@ -16,7 +16,6 @@
 GP = 4
 GB = 4
 VMEM = 60 * 1024 * 1024
-MIDDLE = 40 * 1024 * 1024
 SMALL = 18 * 1024 * 1024
 F32 = jnp.float32
 BF16 = jnp.bfloat16
@@ -198,7 +197,7 @@
             pltpu.VMEM((width, width), BF16),
             pltpu.SemaphoreType.DMA((8,)),
         ],
-        compiler_params=pltpu.CompilerParams(vmem_limit_bytes=MIDDLE),
+        compiler_params=pltpu.CompilerParams(vmem_limit_bytes=VMEM),
         cost_estimate=pl.CostEstimate(
             flops=2 * rows * keys * width * heads * 2, bytes_accessed=20_000_000, transcendentals=rows * keys * heads
         ),
@@ -797,13 +796,13 @@
         small[layer] = (grad_mpre, grad_mpost, grad_gattn, grad_gffn)
 
     total = halve_end(total_kept, total_got)
+    grads, total = after((grads, total))
     got = [swap(send, *core_step) for send in grads[1::2]]
     pieces = [halve_end(keep, g) for keep, g in zip(grads[::2], got)]
     for stage in range(HALVINGS, len(total_order)):
         total_got = swap(total, *total_order[stage])
         pieces, total_got = after((pieces, total_got))
         total = halve_end(total, total_got)
-    own, far = scatter_begin(parts)
     for stage in range(HALVINGS):
         kept, got = zip(*[sum_start(part, order, stage) for part, order in zip(pieces, orders)])
         total_got = swap(total, *total_order[HALVINGS - 1 - stage])
@@ -811,12 +810,9 @@
             got, total_got = after((got, total_got))
             total = spread(total, total_got)
         if stage == HALVINGS - 1:
-            flat_got = flat.start()
-            got, flat_got = after((got, flat_got))
-            flat.end(flat_got)
+            got, far = after((got, far))
         pieces = [halve_end(a, b) for a, b in zip(kept, after(got))]
-        if stage == 0:
-            far, pieces = after((far, pieces))
+        if stage == HALVINGS - 1:
             gn1 = (own + far.astype(F32)).astype(BF16).astype(F32)
             grad_norm, grad_gattn = rms_back(gn1, stream, gain_attn[layer])
             grad_flow = grad_middle + grad_norm
@@ -834,10 +830,13 @@
             flat = Butterfly(flat)
         if stage == 1:
             moving.advance(*pieces)
-            y_parts, pieces = after(([*out_a, *out_b], pieces))
+            y_parts, parts, pieces = after(([*out_a, *out_b], parts, pieces))
+            own, far = scatter_begin(parts)
             own_y, far_y = scatter_begin(y_parts)
     for stage in range(HALVINGS, len(orders[0])):
         got = [swap(part, *order[stage]) for part, order in zip(pieces, orders)]
+        if stage == HALVINGS:
+            flat.end(flat.start())
         flat_got = flat.start()
         if stage == HALVINGS:
             first_rows, second_rows = mirror(grad_flow)

time: 460 us -> 452 us (0.983)
  local copies, waits for them, and re-layouts: 54.9 us -> 46.8 us
  starting transfers between devices: 58.1 us -> 51.9 us
  Pallas kernels: 149 us -> 154 us
    unnamed x308 -> x288, local copies, waits for them, and re-layouts: 31.8 us -> 22.7 us
    ppermute x74, waiting for transfers between devices: 135 us -> 141 us  [swap(): return lax.ppermute(value, axis, [(i, i ^ bit) for i in range(size)])]
  transfers between devices with their start and end apart: 77 -> 77, of which waited for: 34 -> 37; matrix products, arithmetic and copies ran while one was open for 13% -> 13% of each run, Pallas kernels for 26% -> 27%
where the time goes in v1:
time: 452 us; the launch traced here: 443 us
  Pallas kernels  154 us (34%)
  waiting for transfers between devices  146 us (32%)
  starting transfers between devices  51.9 us (11%)
  local copies, waits for them, and re-layouts  46.8 us (10%)
  other arithmetic  41.4 us (9%)
    ppermute x74, waiting for transfers between devices, swap(): return lax.ppermute(value, axis, [(i, i ^ bit) for i in range(size)])  141 us
    pallas_call x2, Pallas kernels, attn_bwd(): pl.pallas_call(functools.partial(attn_bwd_body, heads, blocks, layer, par...  64.3 us
    ppermute x74, starting transfers between devices, swap(): return lax.ppermute(value, axis, [(i, i ^ bit) for i in range(size)])  51.8 us
    pallas_call x2, Pallas kernels, attn_fwd(): pl.pallas_call(functools.partial(attn_fwd_body, blocks, heads, layer, pla...  45.5 us
    unnamed x288, local copies, waits for them, and re-layouts  22.7 us
    pallas_call x4, Pallas kernels, expand(): pl.pallas_call(functools.partial(expand_body, len(halves)), grid_spec=plt...  15.8 us
    convert_element_type x19, other arithmetic, halve_end(): return (kept.astype(F32) + got.astype(F32)).astype(BF16)  14 us
    pallas_call x2, Pallas kernels, ffn_grads(): pl.pallas_call(functools.partial(ffn_grads_body, blocks, chunks), grid=(1...  13.8 us
  transfers between devices with their start and end apart: 77, of which 37 were waited for; matrix products, arithmetic and copies ran while one was open for 13% of the time, Pallas kernels for 27%

profile of v1, /device:TPU:0, one launch (start us, length us, event | category | flops | bytes accessed | tf_op | source)
XLA Modules:
  0.0 443.5 jit_solution(2036740096100044124)
XLA Ops:
  7.8 9.0 %collective-permute-done.1.refs_2_ = bf16[256,768]{1,0:T(8,128)(2,1)S(1)} collective-permute-done((bf16[256,768]{1,0:T(8,128)(2,1)S(1)}, bf16[256,768]{1,0:T(8,128)(2,1)S(1)}, u32[]{:S(2)}, u32[]{:S(2)}) %collective-permute-start.1) | collective-permute-done | bytes 393248 | tf_op jit(solution)/shard_map/ppermute | solution.py:544
  22.4 22.7 %attn_fwd.2 = (bf16[12,256,1024]{2,1,0:T(8,128)(2,1)}, bf16[12,256,768]{2,1,0:T(8,128)(2,1)}, bf16[256,768]{1,0:T(8,128)(2,1)}, bf16[1024,768]{1,0:T(8,128)(2,1)...) custom-call(bf16[256,768]{1,0:T(8,128)(2,1)} %copy-done.109, ...), custom_call_target="tpu_custom_call" | custom-call | flops 9663676416 | bytes 20000000 | tf_op jit(solution)/shard_map/attn_fwd/pallas_call | solution.py:183
  52.3 4.6 %collective-permute-done.6.refs_0_.refs_2_ = bf16[256,768]{1,0:T(8,128)(2,1)S(1)} collective-permute-done((bf16[256,768]{1,0:T(8,128)(2,1)}, bf16[256,768]{1,0:T(8,128)(2,1)S(1)}, u32[]{:S(2)}, u32[]{:S(2)}) %collective-permute-start.6) | collective-permute-done | bytes 393248 | tf_op jit(solution)/shard_map/ppermute | solution.py:544
  63.7 9.8 %collective-permute-done.9 = bf16[256,768]{1,0:T(8,128)(2,1)S(1)} collective-permute-done((bf16[256,768]{1,0:T(8,128)(2,1)S(1)}, bf16[256,768]{1,0:T(8,128)(2,1)S(1)}, u32[]{:S(2)}, u32[]{:S(2)}) %collective-permute-start.9) | collective-permute-done | bytes 393248 | tf_op jit(solution)/shard_map/ppermute | solution.py:544
  76.0 8.9 %collective-permute-done.11.refs_2_ = bf16[256,768]{1,0:T(8,128)(2,1)S(1)} collective-permute-done((bf16[256,768]{1,0:T(8,128)(2,1)S(1)}, bf16[256,768]{1,0:T(8,128)(2,1)S(1)}, u32[]{:S(2)}, u32[]{:S(2)}) %collective-permute-start.11) | collective-permute-done | bytes 393248 | tf_op jit(solution)/shard_map/ppermute | solution.py:544
  87.6 22.9 %attn_fwd.3 = (bf16[12,256,1024]{2,1,0:T(8,128)(2,1)}, bf16[12,256,768]{2,1,0:T(8,128)(2,1)}, bf16[256,768]{1,0:T(8,128)(2,1)}, bf16[1024,768]{1,0:T(8,128)(2,1)...) custom-call(bf16[256,768]{1,0:T(8,128)(2,1)} %copy-done.116, ...), custom_call_target="tpu_custom_call" | custom-call | flops 9663676416 | bytes 20000000 | tf_op jit(solution)/shard_map/attn_fwd/pallas_call | solution.py:183
  134.8 6.9 %ffn_grads.2 = bf16[1536,768]{1,0:T(8,128)(2,1)} custom-call(bf16[256,768]{1,0:T(8,128)(2,1)} %get-tuple-element.209.refs_0_, bf16[256,768]{1,0:T(8,128)(2,1)} %copy-done.30, bf16[256,768]{1,0:T(8,128)(2,1)} %copy-done.31, bf16[256,768]{1,0:T(8,128)(2,1)} %copy-done.32, bf16[256,768]{1,0:T(8,128)(2,1)} %copy-done.7, bf16[256,768]{1,0:T(8,128)(2,1)} %copy-done.6, ...), custom_call_target="tpu_custom_call" | custom-call | flops 2415919104 | bytes 9000000 | tf_op jit(solution)/shard_map/ffn_grads/pallas_call | solution.py:528
  141.7 4.1 collective-permute-done.21
  151.9 32.3 %attn_bwd.2 = (bf16[256,768]{1,0:T(8,128)(2,1)}, bf16[256,768]{1,0:T(8,128)(2,1)}, bf16[256,768]{1,0:T(8,128)(2,1)}, bf16[256,768]{1,0:T(8,128)(2,1)}, bf16[384,...) custom-call(bf16[256,768]{1,0:T(8,128)(2,1)} %get-tuple-element.431.refs_0_, ...), custom_call_target="tpu_custom_call" | custom-call | flops 38654705664 | bytes 20000000 | tf_op jit(solution)/shard_map/attn_bwd/pallas_call | solution.py:347
  192.3 9.9 %collective-permute-done.26 = bf16[384,768]{1,0:T(8,128)(2,1)S(1)} collective-permute-done((bf16[384,768]{1,0:T(8,128)(2,1)S(1)}, bf16[384,768]{1,0:T(8,128)(2,1)S(1)}, u32[]{:S(2)}, u32[]{:S(2)}) %collective-permute-start.26) | collective-permute-done | bytes 589856 | tf_op jit(solution)/shard_map/ppermute | solution.py:544
  210.3 5.4 %collective-permute-done.30.refs_0_.refs_6_ = bf16[256,768]{1,0:T(8,128)(2,1)} collective-permute-done((bf16[256,768]{1,0:T(8,128)(2,1)S(1)}, bf16[256,768]{1,0:T(8,128)(2,1)}, u32[]{:S(2)}, u32[]{:S(2)}) %collective-permute-start.30) | collective-permute-done | bytes 393248 | tf_op jit(solution)/shard_map/ppermute | solution.py:544
  225.9 8.0 %collective-permute-done.34 = bf16[192,3072]{1,0:T(8,128)(2,1)} collective-permute-done((bf16[192,3072]{1,0:T(8,128)(2,1)}, bf16[192,3072]{1,0:T(8,128)(2,1)}, u32[]{:S(2)}, u32[]{:S(2)}) %collective-permute-start.34) | collective-permute-done | bytes 1179680 | tf_op jit(solution)/shard_map/ppermute | solution.py:544
  240.0 7.0 %ffn_grads.3 = bf16[1536,768]{1,0:T(8,128)(2,1)} custom-call(bf16[256,768]{1,0:T(8,128)(2,1)} %get-tuple-element.198.refs_0_, bf16[256,768]{1,0:T(8,128)(2,1)} %copy-done.26, bf16[256,768]{1,0:T(8,128)(2,1)} %copy-done.27, bf16[256,768]{1,0:T(8,128)(2,1)} %copy-done.28, bf16[256,768]{1,0:T(8,128)(2,1)} %copy-done.10, bf16[256,768]{1,0:T(8,128)(2,1)} %copy-done.17, ...), custom_call_target="tpu_custom_call" | custom-call | flops 2415919104 | bytes 9000000 | tf_op jit(solution)/shard_map/ffn_grads/pallas_call | solution.py:528
  257.6 32.1 %attn_bwd.3 = (bf16[256,768]{1,0:T(8,128)(2,1)}, bf16[256,768]{1,0:T(8,128)(2,1)}, bf16[256,768]{1,0:T(8,128)(2,1)}, bf16[256,768]{1,0:T(8,128)(2,1)}, bf16[384,...) custom-call(bf16[256,768]{1,0:T(8,128)(2,1)} %get-tuple-element.427., ...), custom_call_target="tpu_custom_call" | custom-call | flops 38654705664 | bytes 20000000 | tf_op jit(solution)/shard_map/attn_bwd/pallas_call | solution.py:347
  294.9 4.5 %collective-permute-done.41 = bf16[48,3072]{1,0:T(8,128)(2,1)S(1)} collective-permute-done((bf16[48,3072]{1,0:T(8,128)(2,1)S(1)}, bf16[48,3072]{1,0:T(8,128)(2,1)S(1)}, u32[]{:S(2)}, u32[]{:S(2)}) %collective-permute-start.41) | collective-permute-done | bytes 294944 | tf_op jit(solution)/shard_map/ppermute | solution.py:544
  301.4 14.8 %collective-permute-done.44 = bf16[48,3072]{1,0:T(8,128)(2,1)S(1)} collective-permute-done((bf16[48,3072]{1,0:T(8,128)(2,1)S(1)}, bf16[48,3072]{1,0:T(8,128)(2,1)S(1)}, u32[]{:S(2)}, u32[]{:S(2)}) %collective-permute-start.44) | collective-permute-done | bytes 294944 | tf_op jit(solution)/shard_map/ppermute | solution.py:544
  319.4 4.9 %collective-permute-done.45 = bf16[96,1536]{1,0:T(8,128)(2,1)S(1)} collective-permute-done((bf16[96,1536]{1,0:T(8,128)(2,1)S(1)}, bf16[96,1536]{1,0:T(8,128)(2,1)S(1)}, u32[]{:S(2)}, u32[]{:S(2)}) %collective-permute-start.45) | collective-permute-done | bytes 294944 | tf_op jit(solution)/shard_map/ppermute | solution.py:544
  325.4 6.1 %collective-permute-done.47 = bf16[96,3072]{1,0:T(8,128)(2,1)S(1)} collective-permute-done((bf16[96,3072]{1,0:T(8,128)(2,1)S(1)}, bf16[96,3072]{1,0:T(8,128)(2,1)S(1)}, u32[]{:S(2)}, u32[]{:S(2)}) %collective-permute-start.47) | collective-permute-done | bytes 589856 | tf_op jit(solution)/shard_map/ppermute | solution.py:544
  342.6 4.0 collective-permute-done.52
  350.1 8.1 %collective-permute-done.58 = bf16[384,768]{1,0:T(8,128)(2,1)S(1)} collective-permute-done((bf16[384,768]{1,0:T(8,128)(2,1)S(1)}, bf16[384,768]{1,0:T(8,128)(2,1)S(1)}, u32[]{:S(2)}, u32[]{:S(2)}) %collective-permute-start.58) | collective-permute-done | bytes 589856 | tf_op jit(solution)/shard_map/ppermute | solution.py:544
  360.5 7.4 %collective-permute-done.54 = bf16[48,1536]{1,0:T(8,128)(2,1)} collective-permute-done((bf16[48,1536]{1,0:T(8,128)(2,1)S(1)}, bf16[48,1536]{1,0:T(8,128)(2,1)}, u32[]{:S(2)}, u32[]{:S(2)}) %collective-permute-start.54) | collective-permute-done | bytes 147488 | tf_op jit(solution)/shard_map/ppermute | solution.py:544
  407.5 4.9 %expand.5 = (f32[2,768,2304]{2,1,0:T(8,128)}, f32[2,768,768]{2,1,0:T(8,128)}) custom-call(s32[3]{0:T(128)S(1)} %copy-done.34, bf16[384,3072]{1,0:T(8,128)(2,1)} %collective-permute-done.65.refs_0_, f32[2,768,2304]{2,1,0:T(8,128)} %get-tuple-element.358.refs_1_, f32[2,768,768]{2,1,0:T(8,128)} %get-tuple-element.359.refs_2_), custom_call_target="tpu_custom_call", output_to_operand_aliasing={{0}: (2, {}), {1}: (3, {})} | custom-call | bytes 7000000 | tf_op jit(solution)/shard_map/expand/pallas_call | solution.py:410
  412.3 6.4 %collective-permute-done.72 = bf16[192,1536]{1,0:T(8,128)(2,1)} collective-permute-done((bf16[192,1536]{1,0:T(8,128)(2,1)S(1)}, bf16[192,1536]{1,0:T(8,128)(2,1)}, u32[]{:S(2)}, u32[]{:S(2)}) %collective-permute-start.72) | collective-permute-done | bytes 589856 | tf_op jit(solution)/shard_map/ppermute | solution.py:544
  438.5 4.7 %expand.7 = (f32[2,768,2304]{2,1,0:T(8,128)}, f32[2,768,768]{2,1,0:T(8,128)}) custom-call(s32[4]{0:T(128)S(1)} %copy-done.33, bf16[384,1536]{1,0:T(8,128)(2,1)S(1)} %collective-permute-done.75.refs_0_, bf16[384,1536]{1,0:T(8,128)(2,1)} %collective-permute-done.76.refs_1_, ...), custom_call_target="tpu_custom_call", output_to_operand_aliasing={{0}: (3, {}), {1}: (4, {})} | custom-call | bytes 7000000 | tf_op jit(solution)/shard_map/expand/pallas_call | solution.py:410
  (585 shorter events, 191.3 us)
Async XLA Ops:
  3.8 17.7 %collective-permute-start = (bf16[256,768]{1,0:T(8,128)(2,1)S(1)}, bf16[256,768]{1,0:T(8,128)(2,1)S(1)}, u32[]{:S(2)}, u32[]{:S(2)}) collective-permute-start(bf16[256,768]{1,0:T(8,128)(2,1)S(1)} %fusion.30.refs_0_), channel_id=1, source_target_pairs={{0,1},{1,0},{2,3},{3,2},{4,5},{5,4},{6,7},{7,6},{8,9},{9,8},{10,11... | collective-permute-start | bytes 1179656 | tf_op jit(solution)/shard_map/ppermute | solution.py:544
  84.9 25.5 %collective-permute-start.13 = (bf16[256,768]{1,0:T(8,128)(2,1)S(1)}, bf16[256,768]{1,0:T(8,128)(2,1)S(1)}, u32[]{:S(2)}, u32[]{:S(2)}) collective-permute-start(bf16[256,768]{1,0:T(8,128)(2,1)S(1)} %bitcast.105), channel_id=1, source_target_pairs={{0,1},{1,0},{2,3},{3,2},{4,5},{5,4},{6,7},{7,6},{8,9},{9,8},{10,11... | collective-permute-start | bytes 1179656 | tf_op jit(solution)/shard_map/ppermute | solution.py:544
  85.4 25.0 %collective-permute-start.14 = (bf16[256,768]{1,0:T(8,128)(2,1)S(1)}, bf16[256,768]{1,0:T(8,128)(2,1)}, u32[]{:S(2)}, u32[]{:S(2)}) collective-permute-start(bf16[256,768]{1,0:T(8,128)(2,1)S(1)} %bitcast.106), channel_id=1, source_target_pairs={{0,2},{1,3},{2,0},{3,1},{4,6},{5,7},{6,4},{7,5},{8,10},{9,11},{10,... | collective-permute-start | bytes 1179656 | tf_op jit(solution)/shard_map/ppermute | solution.py:544
  149.4 34.8 %collective-permute-start.22 = (bf16[768,768]{1,0:T(8,128)(2,1)}, bf16[768,768]{1,0:T(8,128)(2,1)}, u32[]{:S(2)}, u32[]{:S(2)}) collective-permute-start(bf16[768,768]{1,0:T(8,128)(2,1)} %dynamic-slice_bitcast_fusion.1), channel_id=1, source_target_pairs={{0,4},{4,0},{8,12},{12,8},{16,20},{20,16},{24,28},{28,24},{1,5},{5... | collective-permute-start | bytes 3538952 | tf_op jit(solution)/shard_map/ppermute | solution.py:544
  186.9 15.4 %collective-permute-start.26 = (bf16[384,768]{1,0:T(8,128)(2,1)S(1)}, bf16[384,768]{1,0:T(8,128)(2,1)S(1)}, u32[]{:S(2)}, u32[]{:S(2)}) collective-permute-start(bf16[384,768]{1,0:T(8,128)(2,1)S(1)} %dynamic-slice_bitcast_fusion.3), channel_id=1, source_target_pairs={{0,8},{4,12},{8,0},{12,4},{16,24},{20,28},{24,16},{28,20},{1,9},{5... | collective-permute-start | bytes 1769480 | tf_op jit(solution)/shard_map/ppermute | solution.py:544
  205.3 28.6 %collective-permute-start.34 = (bf16[192,3072]{1,0:T(8,128)(2,1)}, bf16[192,3072]{1,0:T(8,128)(2,1)}, u32[]{:S(2)}, u32[]{:S(2)}) collective-permute-start(bf16[192,3072]{1,0:T(8,128)(2,1)} %slice.199), channel_id=1, source_target_pairs={{0,4},{4,0},{8,12},{12,8},{16,20},{20,16},{24,28},{28,24},{1,5},{5... | collective-permute-start | bytes 3538952 | tf_op jit(solution)/shard_map/ppermute | solution.py:544
  223.3 66.4 %collective-permute-start.38 = (bf16[192,768]{1,0:T(8,128)(2,1)}, bf16[192,768]{1,0:T(8,128)(2,1)}, u32[]{:S(2)}, u32[]{:S(2)}) collective-permute-start(bf16[192,768]{1,0:T(8,128)(2,1)} %dynamic-slice_bitcast_fusion.5), channel_id=1, source_target_pairs={{0,16},{4,20},{8,24},{12,28},{16,0},{20,4},{24,8},{28,12},{1,17},{... | collective-permute-start | bytes 884744 | tf_op jit(solution)/shard_map/ppermute | solution.py:544
  225.9 21.1 %collective-permute-start.29 = (bf16[256,768]{1,0:T(8,128)(2,1)S(1)}, bf16[256,768]{1,0:T(8,128)(2,1)}, u32[]{:S(2)}, u32[]{:S(2)}) collective-permute-start(bf16[256,768]{1,0:T(8,128)(2,1)S(1)} %copy-done.50), channel_id=1, source_target_pairs={{0,1},{1,0},{2,3},{3,2},{4,5},{5,4},{6,7},{7,6},{8,9},{9,8},{10,11... | collective-permute-start | bytes 1179656 | tf_op jit(solution)/shard_map/ppermute | solution.py:544
  238.4 14.5 %collective-permute-start.35 = (bf16[96,3072]{1,0:T(8,128)(2,1)}, bf16[96,3072]{1,0:T(8,128)(2,1)S(1)}, u32[]{:S(2)}, u32[]{:S(2)}) collective-permute-start(bf16[96,3072]{1,0:T(8,128)(2,1)} %slice.201), channel_id=1, source_target_pairs={{0,8},{4,12},{8,0},{12,4},{16,24},{20,28},{24,16},{28,20},{1,9},{5... | collective-permute-start | bytes 1769480 | tf_op jit(solution)/shard_map/ppermute | solution.py:544
  253.8 35.9 %collective-permute-start.36 = (bf16[768,768]{1,0:T(8,128)(2,1)S(1)}, bf16[768,768]{1,0:T(8,128)(2,1)}, u32[]{:S(2)}, u32[]{:S(2)}) collective-permute-start(bf16[768,768]{1,0:T(8,128)(2,1)S(1)} %dynamic-slice_bitcast_fusion), channel_id=1, source_target_pairs={{0,4},{4,0},{8,12},{12,8},{16,20},{20,16},{24,28},{28,24},{1,5},{5... | collective-permute-start | bytes 3538952 | tf_op jit(solution)/shard_map/ppermute | solution.py:544
  254.9 34.7 %collective-permute-start.37 = (bf16[48,3072]{1,0:T(8,128)(2,1)S(1)}, bf16[48,3072]{1,0:T(8,128)(2,1)S(1)}, u32[]{:S(2)}, u32[]{:S(2)}) collective-permute-start(bf16[48,3072]{1,0:T(8,128)(2,1)S(1)} %slice.203), channel_id=1, source_target_pairs={{0,16},{4,20},{8,24},{12,28},{16,0},{20,4},{24,8},{28,12},{1,17},{... | collective-permute-start | bytes 884744 | tf_op jit(solution)/shard_map/ppermute | solution.py:544
  299.4 16.8 %collective-permute-start.42 = (bf16[192,1536]{1,0:T(8,128)(2,1)S(1)}, bf16[192,1536]{1,0:T(8,128)(2,1)S(1)}, u32[]{:S(2)}, u32[]{:S(2)}) collective-permute-start(bf16[192,1536]{1,0:T(8,128)(2,1)S(1)} %slice.172), channel_id=1, source_target_pairs={{0,2},{1,3},{2,0},{3,1},{4,6},{5,7},{6,4},{7,5},{8,10},{9,11},{10,... | collective-permute-start | bytes 1769480 | tf_op jit(solution)/shard_map/ppermute | solution.py:544
  299.8 16.5 %collective-permute-start.43 = (bf16[192,1536]{1,0:T(8,128)(2,1)S(1)}, bf16[192,1536]{1,0:T(8,128)(2,1)S(1)}, u32[]{:S(2)}, u32[]{:S(2)}) collective-permute-start(bf16[192,1536]{1,0:T(8,128)(2,1)S(1)} %slice.173), channel_id=1, source_target_pairs={{0,4},{4,0},{8,12},{12,8},{16,20},{20,16},{24,28},{28,24},{1,5},{5... | collective-permute-start | bytes 1769480 | tf_op jit(solution)/shard_map/ppermute | solution.py:544
  301.0 15.2 %collective-permute-start.44 = (bf16[48,3072]{1,0:T(8,128)(2,1)S(1)}, bf16[48,3072]{1,0:T(8,128)(2,1)S(1)}, u32[]{:S(2)}, u32[]{:S(2)}) collective-permute-start(bf16[48,3072]{1,0:T(8,128)(2,1)S(1)} %add_convert_fusion.20), channel_id=1, source_target_pairs={{0,16},{4,20},{8,24},{12,28},{16,0},{20,4},{24,8},{28,12},{1,17},{... | collective-permute-start | bytes 884744 | tf_op jit(solution)/shard_map/ppermute | solution.py:544
  337.8 31.0 %collective-permute-start.57 = (bf16[192,3072]{1,0:T(8,128)(2,1)S(1)}, bf16[192,3072]{1,0:T(8,128)(2,1)}, u32[]{:S(2)}, u32[]{:S(2)}) collective-permute-start(bf16[192,3072]{1,0:T(8,128)(2,1)S(1)} %pad_maximum_fusion.1), channel_id=1, source_target_pairs={{0,4},{4,0},{8,12},{12,8},{16,20},{20,16},{24,28},{28,24},{1,5},{5... | collective-permute-start | bytes 3538952 | tf_op jit(solution)/shard_map/ppermute | solution.py:544
  339.8 18.4 %collective-permute-start.58 = (bf16[384,768]{1,0:T(8,128)(2,1)S(1)}, bf16[384,768]{1,0:T(8,128)(2,1)S(1)}, u32[]{:S(2)}, u32[]{:S(2)}) collective-permute-start(bf16[384,768]{1,0:T(8,128)(2,1)S(1)} %dynamic-slice_bitcast_fusion.2), channel_id=1, source_target_pairs={{0,8},{4,12},{8,0},{12,4},{16,24},{20,28},{24,16},{28,20},{1,9},{5... | collective-permute-start | bytes 1769480 | tf_op jit(solution)/shard_map/ppermute | solution.py:544
  341.2 19.3 %collective-permute-start.60 = (bf16[256,768]{1,0:T(8,128)(2,1)}, bf16[256,768]{1,0:T(8,128)(2,1)S(1)}, u32[]{:S(2)}, u32[]{:S(2)}) collective-permute-start(bf16[256,768]{1,0:T(8,128)(2,1)} %add_convert_fusion.8), channel_id=1, source_target_pairs={{0,2},{1,3},{2,0},{3,1},{4,6},{5,7},{6,4},{7,5},{8,10},{9,11},{10,... | collective-permute-start | bytes 1179656 | tf_op jit(solution)/shard_map/ppermute | solution.py:544
  350.1 17.9 %collective-permute-start.56 = (f32[128,768]{1,0:T(8,128)}, f32[128,768]{1,0:T(8,128)S(1)}, u32[]{:S(2)}, u32[]{:S(2)}) collective-permute-start(f32[128,768]{1,0:T(8,128)} %get-tuple-element.437), channel_id=1, source_target_pairs={{0,3},{1,2},{2,1},{3,0},{4,7},{5,6},{6,5},{7,4},{8,11},{9,10},{10,... | collective-permute-start | bytes 1179656 | tf_op jit(solution)/shard_map/ppermute | solution.py:684
  370.3 19.7 %collective-permute-start.65 = (bf16[384,3072]{1,0:T(8,128)(2,1)S(1)}, bf16[384,3072]{1,0:T(8,128)(2,1)}, u32[]{:S(2)}, u32[]{:S(2)}) collective-permute-start(bf16[384,3072]{1,0:T(8,128)(2,1)S(1)} %pad_maximum_fusion.refs_0_), channel_id=1, source_target_pairs={{0,1},{1,0},{2,3},{3,2},{4,5},{5,4},{6,7},{7,6},{8,9},{9,8},{10,11... | collective-permute-start | bytes 7077896 | tf_op jit(solution)/shard_map/ppermute | solution.py:544
  388.5 14.3 %collective-permute-start.69 = (bf16[192,768]{1,0:T(8,128)(2,1)S(1)}, bf16[192,768]{1,0:T(8,128)(2,1)S(1)}, u32[]{:S(2)}, u32[]{:S(2)}) collective-permute-start(bf16[192,768]{1,0:T(8,128)(2,1)S(1)} %dynamic-slice_bitcast_fusion.4), channel_id=1, source_target_pairs={{0,16},{4,20},{8,24},{12,28},{16,0},{20,4},{24,8},{28,12},{1,17},{... | collective-permute-start | bytes 884744 | tf_op jit(solution)/shard_map/ppermute | solution.py:544
  403.2 15.5 %collective-permute-start.72 = (bf16[192,1536]{1,0:T(8,128)(2,1)S(1)}, bf16[192,1536]{1,0:T(8,128)(2,1)}, u32[]{:S(2)}, u32[]{:S(2)}) collective-permute-start(bf16[192,1536]{1,0:T(8,128)(2,1)S(1)} %pad_maximum_fusion.5), channel_id=1, source_target_pairs={{0,2},{1,3},{2,0},{3,1},{4,6},{5,7},{6,4},{7,5},{8,10},{9,11},{10,... | collective-permute-start | bytes 1769480 | tf_op jit(solution)/shard_map/ppermute | solution.py:544
  404.5 15.5 %collective-permute-start.73 = (bf16[192,1536]{1,0:T(8,128)(2,1)S(1)}, bf16[192,1536]{1,0:T(8,128)(2,1)S(1)}, u32[]{:S(2)}, u32[]{:S(2)}) collective-permute-start(bf16[192,1536]{1,0:T(8,128)(2,1)S(1)} %pad_maximum_fusion.6), channel_id=1, source_target_pairs={{0,4},{4,0},{8,12},{12,8},{16,20},{20,16},{24,28},{28,24},{1,5},{5... | collective-permute-start | bytes 1769480 | tf_op jit(solution)/shard_map/ppermute | solution.py:544
  406.5 14.2 %collective-permute-start.74 = (f32[8,768]{1,0:T(8,128)S(1)}, f32[8,768]{1,0:T(8,128)S(1)}, u32[]{:S(2)}, u32[]{:S(2)}) collective-permute-start(f32[8,768]{1,0:T(8,128)S(1)} %add.341), channel_id=1, source_target_pairs={{0,16},{4,20},{8,24},{12,28},{16,0},{20,4},{24,8},{28,12},{1,17},{... | collective-permute-start | bytes 73736 | tf_op jit(solution)/shard_map/ppermute | solution.py:544
  422.0 14.3 %collective-permute-start.75 = (bf16[384,1536]{1,0:T(8,128)(2,1)S(1)}, bf16[384,1536]{1,0:T(8,128)(2,1)S(1)}, u32[]{:S(2)}, u32[]{:S(2)}) collective-permute-start(bf16[384,1536]{1,0:T(8,128)(2,1)S(1)} %pad_maximum_fusion.2.refs_0_), channel_id=1, source_target_pairs={{0,1},{1,0},{2,3},{3,2},{4,5},{5,4},{6,7},{7,6},{8,9},{9,8},{10,11... | collective-permute-start | bytes 3538952 | tf_op jit(solution)/shard_map/ppermute | solution.py:544
  (194 other events, 1184.2 us)
